TPU v7x, 256 devices: a whole 4x4x8 slice. The times are simulated.
256 devices in a mesh: dp: 4 (over y_lo, core), seq: 64 (over x, z, y_hi).
Axes of the slice: x: 4, y: 4 (y_hi: 2, y_lo: 2; y = y_hi * 2 + y_lo), z: 8, core: 2. Of those that a mesh axis runs over, the one named last changes fastest.
Arguments:
- inputs: bfloat16 [4, 32768, 1024], P('dp', 'seq'), may hold values from -24 to 24
- w_query: bfloat16 [1024, 1024], replicated, may hold values from -0.1875 to 0.1875
- w_key: bfloat16 [1024, 1024], replicated, may hold values from -0.1875 to 0.1875
- w_value: bfloat16 [1024, 1024], replicated, may hold values from -0.1875 to 0.1875
- key_proj: bfloat16 [256, 32768], P(None, 'seq'), may hold values from -6 to 6
- value_proj: bfloat16 [256, 32768], P(None, 'seq'), may hold values from -6 to 6
- cotangent: bfloat16 [4, 32768, 1024], P('dp', 'seq'), may hold values from -6 to 6
Outputs:
- attended: bfloat16 [4, 32768, 1024], P('dp', 'seq')
- grad_inputs: bfloat16 [4, 32768, 1024], P('dp', 'seq')
- grad_query: float32 [1024, 1024], P('seq')
- grad_key: float32 [1024, 1024], P('seq')
- grad_value: float32 [1024, 1024], P('seq')
All inputs are finite; a program needn't handle non-finite values.
Results may differ from a plain program's by a relative error of at most 0.017.
The roundings to bfloat16 on the way count: a program that leaves them out, or rounds other values in their place, can miss the bound.
Values sent between devices are 32-bit elements; how exact they have to be, the bound alone decides.
No kernel may reach another device: no remote copies, remote signals or barrier semaphores. Data moves between devices by JAX's collectives and lax.ppermute only.
A program may use at most 128 MiB of HBM per device.

v0:
```python
import math

import jax
import jax.numpy as jnp
from jax import lax
from jax.sharding import PartitionSpec as P

HEADS = 16


def body(inputs, w_query, w_key, w_value, key_proj, value_proj, cotangent):
    docs, rows, width = inputs.shape
    head_dim = width // HEADS
    proj_rows = key_proj.shape[0]
    scale = 1.0 / math.sqrt(head_dim)
    n_seq = lax.axis_size("seq")
    n_data = lax.axis_size("dp")
    norm = 1.0 / math.sqrt(rows * n_seq)
    query = jnp.einsum("blc,cd->bld", inputs, w_query, preferred_element_type=jnp.float32).astype(
        jnp.bfloat16
    )
    keys = jnp.einsum("blc,cd->bld", inputs, w_key, preferred_element_type=jnp.float32).astype(
        jnp.bfloat16
    )
    values = jnp.einsum("blc,cd->bld", inputs, w_value, preferred_element_type=jnp.float32).astype(
        jnp.bfloat16
    )
    key_part = jnp.einsum("jl,bld->bjd", key_proj, keys, preferred_element_type=jnp.float32)
    value_part = jnp.einsum("jl,bld->bjd", value_proj, values, preferred_element_type=jnp.float32)
    key_sum, value_sum = lax.psum((key_part, value_part), "seq")
    key_h = (key_sum * norm).astype(jnp.bfloat16).reshape(docs, proj_rows, HEADS, head_dim)
    value_h = (value_sum * norm).astype(jnp.bfloat16).reshape(docs, proj_rows, HEADS, head_dim)
    query_h = query.reshape(docs, rows, HEADS, head_dim)
    upstream_h = cotangent.reshape(docs, rows, HEADS, head_dim)
    scores = (
        jnp.einsum("blhe,bjhe->bhlj", query_h, key_h, preferred_element_type=jnp.float32) * scale
    )
    probs = jax.nn.softmax(scores, axis=-1)
    probs_low = probs.astype(jnp.bfloat16)
    attended = jnp.einsum("bhlj,bjhe->blhe", probs_low, value_h, preferred_element_type=jnp.float32)
    attended = attended.reshape(docs, rows, width).astype(jnp.bfloat16)
    dprob = jnp.einsum("blhe,bjhe->bhlj", upstream_h, value_h, preferred_element_type=jnp.float32)
    dscore = (probs * (dprob - jnp.sum(probs * dprob, axis=-1, keepdims=True)) * scale).astype(
        jnp.bfloat16
    )
    dquery = jnp.einsum("bhlj,bjhe->blhe", dscore, key_h, preferred_element_type=jnp.float32)
    dquery = dquery.reshape(docs, rows, width).astype(jnp.bfloat16)
    dkp_part = jnp.einsum("bhlj,blhe->bjhe", dscore, query_h, preferred_element_type=jnp.float32)
    dvp_part = jnp.einsum(
        "bhlj,blhe->bjhe", probs_low, upstream_h, preferred_element_type=jnp.float32
    )
    dkp_sum, dvp_sum = lax.psum(
        (dkp_part.reshape(docs, proj_rows, width), dvp_part.reshape(docs, proj_rows, width)), "seq"
    )
    dkp_low = (dkp_sum * norm).astype(jnp.bfloat16)
    dvp_low = (dvp_sum * norm).astype(jnp.bfloat16)
    dkeys = jnp.einsum("jl,bjd->bld", key_proj, dkp_low, preferred_element_type=jnp.float32).astype(
        jnp.bfloat16
    )
    dvalues = jnp.einsum(
        "jl,bjd->bld", value_proj, dvp_low, preferred_element_type=jnp.float32
    ).astype(jnp.bfloat16)
    grad_in = jnp.einsum("bld,cd->blc", dquery, w_query, preferred_element_type=jnp.float32)
    grad_in = grad_in + jnp.einsum("bld,cd->blc", dkeys, w_key, preferred_element_type=jnp.float32)
    grad_in = grad_in + jnp.einsum(
        "bld,cd->blc", dvalues, w_value, preferred_element_type=jnp.float32
    )
    grad_inputs = grad_in.astype(jnp.bfloat16)
    stacked = jnp.concatenate([dquery, dkeys, dvalues], axis=2)
    factor = 1.0 / math.sqrt(docs * rows * n_seq * n_data)
    share = lax.psum_scatter(
        jnp.einsum("blc,bld->cd", inputs, stacked, preferred_element_type=jnp.float32) * factor,
        "seq",
        scatter_dimension=0,
        tiled=True,
    )
    summed = lax.psum(share, "dp")
    grad_query = summed[:, :width]
    grad_key = summed[:, width : 2 * width]
    grad_value = summed[:, 2 * width :]
    return (attended, grad_inputs, grad_query, grad_key, grad_value)


def solution(mesh):
    return jax.shard_map(
        body,
        mesh=mesh,
        in_specs=(
            P("dp", "seq", None),
            P(),
            P(),
            P(),
            P(None, "seq"),
            P(None, "seq"),
            P("dp", "seq", None),
        ),
        out_specs=(
            P("dp", "seq", None),
            P("dp", "seq", None),
            P("seq", None),
            P("seq", None),
            P("seq", None),
        ),
        check_vma=False,
    )
```

profile of v0, /device:TPU:1, one launch (start us, length us, event | category | flops | bytes accessed | tf_op | source)
XLA Modules:
  0.0 2372.2 jit_solution(12891678308620625770)
XLA Ops:
  7.2 4.6 convolution_bitcast_fusion
  11.8 4.1 convolution_bitcast_fusion.1
  17.7 3.5 convolution_convert_fusion.3
  21.2 2.3 copy.34
  23.5 650.3 %all-reduce.10.cloned.1.call-done = (f32[1,256,1024]{1,2,0:T(8,128)}, f32[1,256,1024]{1,2,0:T(8,128)}) async-done(((f32[1,256,1024]{1,2,0:T(8,128)}, f32[1,256,1024]{1,2,0:T(8,128)}), (f32[1,256,1024]{1,2,0:T(8,128)}, f32[1,256,1024]{1,2,0:T(8,128)})) %all-reduce.10.cloned.1.call-update) | async-done | bytes 2097168 | tf_op jit(solution)/shard_map/psum | solution.py:30
  673.8 2.6 multiply_convert_fusion.2
  677.2 4.5 fusion.54
  681.7 7.4 fusion.53
  689.1 5.8 fusion.16
  694.9 15.1 fusion.10
  710.3 14.7 fusion.23
  725.0 680.8 %all-reduce.8.cloned.1.call-done = (f32[1,256,1024]{1,2,0:T(8,128)}, f32[1,256,1024]{1,2,0:T(8,128)}) async-done(((f32[1,256,1024]{1,2,0:T(8,128)}, f32[1,256,1024]{1,2,0:T(8,128)}), (f32[1,256,1024]{1,2,0:T(8,128)}, f32[1,256,1024]{1,2,0:T(8,128)})) %all-reduce.8.cloned.1.call-update) | async-done | bytes 2097168 | tf_op jit(solution)/shard_map/psum | solution.py:52
  1407.5 2.0 convolution_convert_fusion
  1410.5 9.4 multiply_bitcast_fusion
  1419.9 12.6 copy.48
  1433.6 5.2 fusion.20
  1438.8 2.3 copy.40
  1441.1 4.0 fusion.55
  1445.1 3.9 fusion.26
  1449.0 851.4 %reduce-scatter.4.cloned.1.call-done = f32[16,3072]{1,0:T(8,128)} async-done(((f32[1024,3072]{1,0:T(8,128)}), f32[16,3072]{1,0:T(8,128)}) %reduce-scatter.4.cloned.1.call-update) | async-done | bytes 196624
  2300.4 2.6 copy.49
  2303.0 5.1 fusion.24
  2308.1 51.8 %all-reduce.6.cloned.1.call-done = f32[16,3072]{0,1:T(8,128)} async-done(((f32[16,3072]{0,1:T(8,128)}), f32[16,3072]{0,1:T(8,128)}) %all-reduce.6.cloned.1.call-update) | async-done | bytes 196624 | tf_op jit(solution)/shard_map/psum | solution.py:77
  2359.9 2.3 fusion.52
  (35 shorter events, 10.0 us)
Async XLA Ops:
  7.2 10.5 copy-start
  7.2 4.6 copy-start.10
  7.2 4.6 copy-start.8
  7.2 666.6 %all-reduce.10.cloned.1.call-start = ((), (), s32[]{:S(2)}) async-start(), calls=%async_computation.4 | async-start | bytes 4194304 | tf_op jit(solution)/shard_map/psum | solution.py:30
  15.9 1389.9 %all-reduce.8.cloned.1.call-start = ((), (), s32[]{:S(2)}) async-start(), calls=%async_computation.3 | async-start | bytes 4194304 | tf_op jit(solution)/shard_map/psum | solution.py:52
  676.4 0.8 copy-start.1
  694.9 15.4 copy-start.6
  710.0 695.8 %copy-start.7 = (bf16[256,512]{1,0:T(8,128)(2,1)S(1)}, bf16[256,512]{1,0:T(8,128)(2,1)}, u32[]{:S(2)}) copy-start(bf16[256,512]{1,0:T(8,128)(2,1)} %param.11) | copy-start | bytes 786436
  710.0 1590.4 %reduce-scatter.4.cloned.1.call-start = ((), (), s32[]{:S(2)}) async-start(), calls=%async_computation.2 | async-start | bytes 12779520
  1407.5 2.1 copy-start.5
  1409.5 1.0 copy-start.3
  1432.5 1.0 copy-start.2
  1432.6 927.3 %all-reduce.6.cloned.1.call-start = ((), (), s32[]{:S(2)}) async-start(), calls=%async_computation.1 | async-start | bytes 3145728 | tf_op jit(solution)/shard_map/psum | solution.py:77
  1441.1 4.0 copy-start.9
  1445.1 857.9 %copy-start.4 = (bf16[1024,512]{1,0:T(8,128)(2,1)S(1)}, bf16[1024,512]{1,0:T(8,128)(2,1)}, u32[]{:S(2)}) copy-start(bf16[1024,512]{1,0:T(8,128)(2,1)} %copy-done.3) | copy-start | bytes 3145732
Sparse Core Ops, SparseCore 0:
  16.1 657.6 all-reduce.9
  710.1 695.6 all-reduce.7
  1432.7 867.6 reduce-scatter.3
  2303.1 56.7 all-reduce.5
where the time goes:
time: 2370 us
  waiting for transfers between devices  2230 us (94%)
  matrix products  91.1 us (4%)
  local copies, waits for them, and re-layouts  29.5 us (1%)
    unnamed x5, waiting for transfers between devices  851 us
    psum x1, waiting for transfers between devices, body(): lax.psum((dkp_part.reshape(docs, proj_rows, width), dvp_part.reshape(docs...  681 us
    psum x1, waiting for transfers between devices, body(): key_sum, value_sum = lax.psum((key_part, value_part), 'seq')  650 us
    psum x1, waiting for transfers between devices, body(): summed = lax.psum(share, 'dp')  51.8 us
  transfers between devices with their start and end apart: 4, of which 4 were waited for; matrix products, arithmetic and copies ran while one was open for 2% of the time, Pallas kernels for 0%

commit v1 on v0

v1 whole, which is shorter than its diff:
```python
import math

import jax
import jax.numpy as jnp
from jax import lax
from jax.sharding import Mesh
from jax.sharding import PartitionSpec as P

HEADS = 16
SPLITS = {64: (4, 8, 2), 8: (2, 2, 2)}
SEQ = ("x", "z", "yh")


def bf16_dot(spec, a, b):
    return jnp.einsum(spec, a, b, preferred_element_type=jnp.float32)


def scatter_sum(part):
    rows, width = part.shape
    plane = lax.axis_size(("x", "yh"))
    depth = lax.axis_size("z")
    got = lax.all_to_all(part.reshape(plane, rows // plane, width), ("x", "yh"), 0, 0)
    mine = jnp.sum(got, axis=0)
    got = lax.all_to_all(mine.reshape(depth, rows // plane // depth, width), "z", 0, 0)
    return jnp.sum(got, axis=0)


def gather_rows(mine):
    rows, width = mine.shape
    plane = lax.axis_size(("x", "yh"))
    depth = lax.axis_size("z")
    got = lax.all_to_all(jnp.broadcast_to(mine, (depth, rows, width)), "z", 0, 0)
    got = got.reshape(depth * rows, width)
    got = lax.all_to_all(jnp.broadcast_to(got, (plane, depth * rows, width)), ("x", "yh"), 0, 0)
    return got.reshape(plane * depth * rows, width)


def by_z(part):
    rows, width = part.shape
    n_x, n_z, n_yh = (lax.axis_size(a) for a in SEQ)
    block = rows // (n_x * n_z * n_yh)
    part = part.reshape(n_x, n_z, n_yh * block, width)
    return jnp.swapaxes(part, 0, 1).reshape(rows, width)


def scatter_rows(part, axes):
    for axis in axes:
        part = lax.psum_scatter(part, axis, scatter_dimension=0, tiled=True)
    return part


def pair_sum(part, axis):
    return part + lax.ppermute(part, axis, [(0, 1), (1, 0)])


def body(inputs, w_query, w_key, w_value, key_proj, value_proj, cotangent):
    inputs, cotangent = inputs[0], cotangent[0]
    rows, width = inputs.shape
    head_dim = width // HEADS
    proj_rows = key_proj.shape[0]
    scale = 1.0 / math.sqrt(head_dim)
    n_seq = lax.axis_size(SEQ)
    n_data = lax.axis_size(("yl", "core"))
    norm = 1.0 / math.sqrt(rows * n_seq)
    factor = 1.0 / math.sqrt(rows * n_seq * n_data)

    keys = bf16_dot("lc,cd->ld", inputs, w_key).astype(jnp.bfloat16)
    values = bf16_dot("lc,cd->ld", inputs, w_value).astype(jnp.bfloat16)
    key_part = bf16_dot("jl,ld->jd", key_proj, keys)
    value_part = bf16_dot("jl,ld->jd", value_proj, values)
    sums = gather_rows(scatter_sum(jnp.concatenate([key_part, value_part], axis=0)))

    both_proj = jnp.concatenate([key_proj, value_proj], axis=0)
    seen = by_z(bf16_dot("lc,jl->cj", inputs, both_proj))
    seen = scatter_rows(seen, ("z", "x", "yh"))

    query = bf16_dot("lc,cd->ld", inputs, w_query).astype(jnp.bfloat16)
    low = (sums * norm).astype(jnp.bfloat16)
    key_h = low[:proj_rows].reshape(proj_rows, HEADS, head_dim)
    value_h = low[proj_rows:].reshape(proj_rows, HEADS, head_dim)
    query_h = query.reshape(rows, HEADS, head_dim)
    upstream_h = cotangent.reshape(rows, HEADS, head_dim)
    scores = bf16_dot("lhe,jhe->hlj", query_h, key_h) * scale
    probs = jax.nn.softmax(scores, axis=-1)
    probs_low = probs.astype(jnp.bfloat16)
    attended = bf16_dot("hlj,jhe->lhe", probs_low, value_h)
    attended = attended.reshape(rows, width).astype(jnp.bfloat16)
    dprob = bf16_dot("lhe,jhe->hlj", upstream_h, value_h)
    dscore = (probs * (dprob - jnp.sum(probs * dprob, axis=-1, keepdims=True)) * scale).astype(
        jnp.bfloat16
    )
    dquery = bf16_dot("hlj,jhe->lhe", dscore, key_h).reshape(rows, width).astype(jnp.bfloat16)
    dkp_part = bf16_dot("hlj,lhe->jhe", dscore, query_h).reshape(proj_rows, width)
    dvp_part = bf16_dot("hlj,lhe->jhe", probs_low, upstream_h).reshape(proj_rows, width)

    dquery_blocks = dquery.reshape(rows, n_data, width // n_data)
    grad_q = jnp.stack(
        [bf16_dot("lc,ld->cd", inputs, dquery_blocks[:, p]) for p in range(n_data)]
    )
    grad_q = grad_q.reshape(2, 2 * width, width // n_data)
    grad_q = jnp.sum(lax.all_to_all(grad_q, "core", 0, 0), axis=0)
    grad_q = jnp.concatenate([by_z(grad_q[:width]), by_z(grad_q[width:])], axis=1)
    grad_q = scatter_rows(grad_q, ("z", "x", "yh"))
    grad_q = jnp.stack([grad_q[:, : width // n_data], grad_q[:, width // n_data :]])
    grad_q = lax.psum_scatter(grad_q, "yl", scatter_dimension=0)

    sums = gather_rows(scatter_sum(jnp.concatenate([dkp_part, dvp_part], axis=0)))
    low = (sums * norm).astype(jnp.bfloat16)
    dkp_low, dvp_low = low[:proj_rows], low[proj_rows:]
    seen_high = seen.astype(jnp.bfloat16)
    seen_low = (seen - seen_high.astype(jnp.float32)).astype(jnp.bfloat16)
    grad_k = bf16_dot("cj,jd->cd", seen_high[:, :proj_rows], dkp_low)
    grad_k = grad_k + bf16_dot("cj,jd->cd", seen_low[:, :proj_rows], dkp_low)
    grad_v = bf16_dot("cj,jd->cd", seen_high[:, proj_rows:], dvp_low)
    grad_v = grad_v + bf16_dot("cj,jd->cd", seen_low[:, proj_rows:], dvp_low)
    place = lax.axis_index("core") * 2 + lax.axis_index("yl")
    column = lax.broadcasted_iota(jnp.int32, (1, n_data, 1), 1)
    grad_q = jnp.where(column == place, grad_q[:, None, :], 0.0).reshape(-1, width)
    grads = jnp.concatenate([grad_q, grad_k, grad_v], axis=0) * factor
    grads = pair_sum(pair_sum(grads, "core"), "yl")
    grad_q, grad_k, grad_v = jnp.split(grads, 3, axis=0)

    dkeys = bf16_dot("jl,jd->ld", key_proj, dkp_low).astype(jnp.bfloat16)
    dvalues = bf16_dot("jl,jd->ld", value_proj, dvp_low).astype(jnp.bfloat16)
    grad_in = bf16_dot("ld,cd->lc", dquery, w_query)
    grad_in = grad_in + bf16_dot("ld,cd->lc", dkeys, w_key)
    grad_in = grad_in + bf16_dot("ld,cd->lc", dvalues, w_value)
    grad_inputs = grad_in.astype(jnp.bfloat16)
    return (attended[None], grad_inputs[None], grad_q, grad_k, grad_v)


def solution(mesh):
    split = SPLITS[mesh.shape["seq"]]
    fine = Mesh(mesh.devices.reshape((2, 2) + split), ("yl", "core") + SEQ)
    tokens = P(("yl", "core"), SEQ, None)
    return jax.shard_map(
        body,
        mesh=fine,
        in_specs=(tokens, P(), P(), P(), P(None, SEQ), P(None, SEQ), tokens),
        out_specs=(tokens, tokens, P(SEQ, None), P(SEQ, None), P(SEQ, None)),
        check_vma=False,
    )
```

time: 2370 us -> 388 us (0.16)
  waiting for transfers between devices: 2230 us -> 120 us
  blocking collectives: 0 us -> 66.5 us
  starting transfers between devices: 0.83 us -> 32.2 us
    psum x3 -> x0, waiting for transfers between devices: 1380 us -> none  [the longest x1 681 us: body(): lax.psum((dkp_part.reshape(docs, proj_rows, width), dvp_part.reshape(docs...]
    unnamed x5 -> x7, waiting for transfers between devices: 851 us -> 0.12 us
    all_to_all x0 -> x5, waiting for transfers between devices: none -> 81.9 us  [the longest x2 42.7 us: scatter_sum(): lax.all_to_all(part.reshape(plane, rows // plane, width), ('x', 'yh'), 0, 0)]
    all_to_all x0 -> x4, blocking collectives: none -> 66.5 us  [the longest x2 38.6 us: scatter_sum(): lax.all_to_all(mine.reshape(depth, rows // plane // depth, width), 'z', 0...]
    reduce_scatter x0 -> x7, waiting for transfers between devices: none -> 37.2 us  [the longest x6 21.4 us: scatter_rows(): part = lax.psum_scatter(part, axis, scatter_dimension=0, tiled=True)]
    all_to_all x0 -> x5, starting transfers between devices: none -> 30.1 us  [the longest x2 11.8 us: scatter_sum(): lax.all_to_all(part.reshape(plane, rows // plane, width), ('x', 'yh'), 0, 0)]
    dot_general x14 -> x20, matrix products: 83.7 us -> 77.8 us  [bf16_dot(): return jnp.einsum(spec, a, b, preferred_element_type=jnp.float32)]
  transfers between devices with their start and end apart: 4 -> 14, of which waited for: 4 -> 9; matrix products, arithmetic and copies ran while one was open for 2% -> 36% of each run, Pallas kernels for 0% -> 0%
where the time goes in v1:
time: 388 us; the launch traced here: 386 us
  waiting for transfers between devices  120 us (31%)
  matrix products  85.2 us (22%)
  blocking collectives  66.5 us (17%)
  local copies, waits for them, and re-layouts  42.4 us (11%)
  starting transfers between devices  32.2 us (8%)
  other arithmetic  25.8 us (7%)
  between operations  14.4 us (4%)
    dot_general x20, matrix products, bf16_dot(): return jnp.einsum(spec, a, b, preferred_element_type=jnp.float32)  77.8 us
    all_to_all x2, waiting for transfers between devices, scatter_sum(): lax.all_to_all(part.reshape(plane, rows // plane, width), ('x', 'yh'), 0, 0)  42.7 us
    all_to_all x2, blocking collectives, scatter_sum(): lax.all_to_all(mine.reshape(depth, rows // plane // depth, width), 'z', 0...  38.6 us
    all_to_all x2, waiting for transfers between devices, gather_rows(): lax.all_to_all(jnp.broadcast_to(got, (plane, depth * rows, width)), ('x',...  37.9 us
    all_to_all x2, blocking collectives, gather_rows(): lax.all_to_all(jnp.broadcast_to(mine, (depth, rows, width)), 'z', 0, 0)  27.9 us
    reduce_scatter x6, waiting for transfers between devices, scatter_rows(): part = lax.psum_scatter(part, axis, scatter_dimension=0, tiled=True)  21.4 us
    reduce_scatter x1, waiting for transfers between devices, body(): grad_q = lax.psum_scatter(grad_q, 'yl', scatter_dimension=0)  15.8 us
    all_to_all x2, starting transfers between devices, scatter_sum(): lax.all_to_all(part.reshape(plane, rows // plane, width), ('x', 'yh'), 0, 0)  11.8 us
  transfers between devices with their start and end apart: 14, of which 9 were waited for; matrix products, arithmetic and copies ran while one was open for 36% of the time, Pallas kernels for 0%

profile of v1, /device:TPU:1, one launch (start us, length us, event | category | flops | bytes accessed | tf_op | source)
XLA Modules:
  0.0 386.2 jit_solution(4952515961490530118)
XLA Ops:
  7.2 4.6 %convolution_bitcast_fusion.2 = f32[256,1024]{1,0:T(8,128)} fusion(bf16[256,512]{1,0:T(8,128)(2,1)} %param.11, bf16[1024,1024]{1,0:T(8,128)(2,1)} %param.9, bf16[1,512,1024]{2,1,0:T(8,128)(2,1)} %param.7), kind=kOutput, calls=%fused_computation.36 | convolution fusion | flops 1342701568 | bytes 4456448 | tf_op jit(solution)/shard_map/jl,ld->jd/dot_general | solution.py:15
  19.1 7.5 %all-to-all-start = ((f32[8,64,1024]{2,1,0:T(8,128)}), f32[8,64,1024]{2,1,0:T(8,128)}, u32[]{:S(2)}, u32[]{:S(2)}) async-start(f32[8,64,1024]{2,1,0:T(8,128)} %bitcast.155), calls=%async_computation | async-start | bytes 4194304 | tf_op jit(solution)/shard_map/all_to_all | solution.py:22
  35.8 21.4 %all-to-all-done = f32[8,64,1024]{2,1,0:T(8,128)} async-done(((f32[8,64,1024]{2,1,0:T(8,128)}), f32[8,64,1024]{2,1,0:T(8,128)}, u32[]{:S(2)}, u32[]{:S(2)}) %all-to-all-start) | async-done | bytes 2097184 | tf_op jit(solution)/shard_map/all_to_all | solution.py:22
  59.0 21.8 %all_to_all.45 = f32[8,8,1024]{2,1,0:T(8,128)} all-to-all(f32[8,8,1024]{2,1,0:T(8,128)S(1)} %bitcast.174), channel_id=1, replica_groups=mesh['yl'=2,'core'=2,'x'=4,'z'=8,'yh'=2] {'z'}, dimensions={0} | all-to-all | bytes 524288 | tf_op jit(solution)/shard_map/all_to_all | solution.py:24
  81.7 11.8 %all_to_all.46 = f32[8,8,1024]{2,1,0:T(8,128)S(1)} all-to-all(f32[8,8,1024]{2,1,0:T(8,128)S(1)} %broadcast_in_dim.47), channel_id=1, replica_groups=mesh['yl'=2,'core'=2,'x'=4,'z'=8,'yh'=2] {'z'}, dimensions={0} | all-to-all | bytes 524288 | tf_op jit(solution)/shard_map/all_to_all | solution.py:32
  95.1 4.4 %all-to-all-start.3 = ((f32[8,64,1024]{2,1,0:T(8,128)}), f32[8,64,1024]{2,1,0:T(8,128)}, u32[]{:S(2)}, u32[]{:S(2)}) async-start(f32[8,64,1024]{2,1,0:T(8,128)} %broadcast_in_dim.48), calls=%async_computation.3 | async-start | bytes 4194304 | tf_op jit(solution)/shard_map/all_to_all | solution.py:34
  106.4 21.5 %all-to-all-done.3 = f32[8,64,1024]{2,1,0:T(8,128)} async-done(((f32[8,64,1024]{2,1,0:T(8,128)}), f32[8,64,1024]{2,1,0:T(8,128)}, u32[]{:S(2)}, u32[]{:S(2)}) %all-to-all-start.3) | async-done | bytes 2097184 | tf_op jit(solution)/shard_map/all_to_all | solution.py:34
  141.3 5.9 %fusion.55 = f32[16,256,512]{2,1,0:T(8,128)} fusion(bf16[256,16,64]{0,2,1:T(8,128)(2,1)} %copy.57, bf16[512,16,64]{0,2,1:T(8,128)(2,1)} %bitcast.163), kind=kOutput, calls=%fused_computation.85 | convolution fusion | flops 268435456 | bytes 9961472 | tf_op jit(solution)/shard_map/lhe,jhe->hlj/dot_general | solution.py:15
  147.2 7.4 %fusion.54 = (f32[16,512]{1,0:T(8,128)S(1)}, f32[16,512,256]{1,2,0:T(8,128)}) fusion(bf16[512,16,64]{0,2,1:T(8,128)(2,1)} %bitcast.178, bf16[256,16,64]{0,2,1:T(8,128)(2,1)} %copy.56), kind=kOutput, calls=%fused_computation.84 | convolution fusion | flops 274727168 | bytes 9994240 | tf_op jit(solution)/shard_map/sub | solution.py:84
  154.6 15.1 %fusion.10 = f32[16,64,256]{2,1,0:T(8,128)} fusion(bf16[512,16,64]{0,2,1:T(8,128)(2,1)} %bitcast.179, f32[16,256,512]{2,1,0:T(8,128)} %fusion.55, f32[16,512,256]{1,2,0:T(8,128)} %get-tuple-element.39, f32[16,512]{1,0:T(8,128)S(1)} %get-tuple-element.38), kind=kOutput, calls=%fused_computation.14 | convolution fusion | flops 283123968 | bytes 18907136 | tf_op jit(solution)/shard_map/hlj,lhe->jhe/dot_general | solution.py:15
  169.7 14.8 %fusion.19 = bf16[16,64,512]{2,1,0:T(8,128)(2,1)} fusion(bf16[256,16,64]{0,2,1:T(8,128)(2,1)} %copy.56, f32[16,256,512]{2,1,0:T(8,128)} %fusion.55, f32[16,512,256]{1,2,0:T(8,128)} %get-tuple-element.39, f32[16,512]{1,0:T(8,128)S(1)} %get-tuple-element.38), kind=kOutput, calls=%fused_computation.28 | convolution fusion | flops 283648256 | bytes 18382848 | tf_op jit(solution)/shard_map/hlj,jhe->lhe/dot_general | solution.py:15
  184.6 6.1 %fusion.12 = f32[16,256,64]{1,2,0:T(8,128)} fusion(bf16[512,16,64]{0,2,1:T(8,128)(2,1)} %bitcast.164, f32[16,512,256]{1,2,0:T(8,128)} %get-tuple-element.39, f32[16,512]{1,0:T(8,128)S(1)} %get-tuple-element.38), kind=kOutput, calls=%fused_computation.21 | convolution fusion | flops 272629760 | bytes 10518528 | tf_op jit(solution)/shard_map/hlj,lhe->jhe/dot_general | solution.py:15
  199.1 5.4 %copy.67 = f32[4,1024,256]{2,1,0:T(8,128)} copy(f32[4,1024,256]{1,2,0:T(8,128)} %pad_maximum_fusion) | data formatting | bytes 8388608 | tf_op jit(solution)/shard_map/stack | solution.py:97
  204.5 9.5 %all-to-all-start.8 = ((f32[2,2048,256]{2,1,0:T(8,128)}), f32[2,2048,256]{2,1,0:T(8,128)}, u32[]{:S(2)}, u32[]{:S(2)}) async-start(f32[2,2048,256]{2,1,0:T(8,128)} %bitcast.152), calls=%async_computation.8 | async-start | bytes 8388608 | tf_op jit(solution)/shard_map/all_to_all | solution.py:101
  232.4 21.3 %all-to-all-done.4 = f32[8,64,1024]{2,1,0:T(8,128)} async-done(((f32[8,64,1024]{2,1,0:T(8,128)}), f32[8,64,1024]{2,1,0:T(8,128)}, u32[]{:S(2)}, u32[]{:S(2)}) %all-to-all-start.4) | async-done | bytes 2097184 | tf_op jit(solution)/shard_map/all_to_all | solution.py:22
  255.5 16.8 %all_to_all.47 = f32[8,8,1024]{2,1,0:T(8,128)S(1)} all-to-all(f32[8,8,1024]{2,1,0:T(8,128)S(1)} %bitcast.176), channel_id=1, replica_groups=mesh['yl'=2,'core'=2,'x'=4,'z'=8,'yh'=2] {'z'}, dimensions={0} | all-to-all | bytes 524288 | tf_op jit(solution)/shard_map/all_to_all | solution.py:24
  272.3 16.0 %all_to_all.48 = f32[8,8,1024]{2,1,0:T(8,128)S(1)} all-to-all(f32[8,8,1024]{2,1,0:T(8,128)S(1)} %broadcast_in_dim.49), channel_id=1, replica_groups=mesh['yl'=2,'core'=2,'x'=4,'z'=8,'yh'=2] {'z'}, dimensions={0} | all-to-all | bytes 524288 | tf_op jit(solution)/shard_map/all_to_all | solution.py:32
  290.0 4.4 %all-to-all-start.7 = ((f32[8,64,1024]{2,1,0:T(8,128)}), f32[8,64,1024]{2,1,0:T(8,128)}, u32[]{:S(2)}, u32[]{:S(2)}) async-start(f32[8,64,1024]{2,1,0:T(8,128)} %broadcast_in_dim.50), calls=%async_computation.7 | async-start | bytes 4194304 | tf_op jit(solution)/shard_map/all_to_all | solution.py:34
  294.5 5.2 %fusion.16 = bf16[16,64,512]{2,1,0:T(8,128)(2,1)} fusion(bf16[256,16,64]{0,2,1:T(8,128)(2,1)S(1)} %copy-done.2, f32[16,512,256]{1,2,0:T(8,128)} %get-tuple-element.39, f32[16,512]{1,0:T(8,128)S(1)} %get-tuple-element.38), kind=kOutput, calls=%fused_computation.27 | convolution fusion | flops 273154048 | bytes 9994240 | tf_op jit(solution)/shard_map/hlj,jhe->lhe/dot_general | solution.py:15
  306.8 16.3 %all-to-all-done.7 = f32[8,64,1024]{2,1,0:T(8,128)} async-done(((f32[8,64,1024]{2,1,0:T(8,128)}), f32[8,64,1024]{2,1,0:T(8,128)}, u32[]{:S(2)}, u32[]{:S(2)}) %all-to-all-start.7) | async-done | bytes 2097184 | tf_op jit(solution)/shard_map/all_to_all | solution.py:34
  328.6 18.5 %reduce-scatter.12.cloned.1.call-done = f32[16,512]{1,0:T(8,128)} async-done(((f32[32,512]{1,0:T(8,128)}), f32[16,512]{1,0:T(8,128)}) %reduce-scatter.12.cloned.1.call-update) | async-done | bytes 32784 | tf_op jit(solution)/shard_map/reduce_scatter | solution.py:48
  348.7 15.8 %reduce-scatter.14.cloned.1.call-done = f32[1,16,256]{2,1,0:T(8,128)} async-done(((f32[2,16,256]{2,1,0:T(8,128)}), f32[1,16,256]{2,1,0:T(8,128)}) %reduce-scatter.14.cloned.1.call-update) | async-done | bytes 16400 | tf_op jit(solution)/shard_map/reduce_scatter | solution.py:105
  366.6 4.5 %fusion.21 = f32[512,1024]{1,0:T(8,128)} fusion(bf16[1024,1024]{1,0:T(8,128)(2,1)} %param.9, bf16[256,1024]{1,0:T(8,128)(2,1)S(1)} %bitcast.162, bf16[256,512]{1,0:T(8,128)(2,1)} %param.11), kind=kOutput, calls=%fused_computation.41 | convolution fusion | flops 1342701568 | bytes 4980736 | tf_op jit(solution)/shard_map/ld,cd->lc/dot_general | solution.py:15
  372.7 5.5 %fusion.20 = bf16[1,512,1024]{2,1,0:T(8,128)(2,1)} fusion(bf16[1024,1024]{1,0:T(8,128)(2,1)} %param.10, f32[512,1024]{1,0:T(8,128)} %fusion.56, f32[512,1024]{1,0:T(8,128)} %fusion.21, bf16[256,1024]{1,0:T(8,128)(2,1)S(1)} %bitcast.159, bf16[256,512]{1,0:T(8,128)(2,1)} %param.12), kind=kOutput, calls=%fused_computation.34 | convolution fusion | flops 1344274432 | bytes 8126464 | tf_op jit(solution)/shard_map/ld,cd->lc/dot_general | solution.py:15
  (93 shorter events, 90.2 us)
Async XLA Ops:
  7.2 94.7 %copy-start = (bf16[1024,1024]{1,0:T(8,128)(2,1)S(1)}, bf16[1024,1024]{1,0:T(8,128)(2,1)}, u32[]{:S(2)}) copy-start(bf16[1024,1024]{1,0:T(8,128)(2,1)} %param.8) | copy-start | bytes 6291460
  7.2 4.7 %copy-start.1 = (bf16[1,512,1024]{2,1,0:T(8,128)(2,1)S(1)}, bf16[1,512,1024]{2,1,0:T(8,128)(2,1)}, u32[]{:S(2)}) copy-start(bf16[1,512,1024]{2,1,0:T(8,128)(2,1)} %param.7) | copy-start | bytes 3145732
  7.2 4.7 %copy-start.5 = (bf16[256,512]{1,0:T(8,128)(2,1)S(1)}, bf16[256,512]{1,0:T(8,128)(2,1)}, u32[]{:S(2)}) copy-start(bf16[256,512]{1,0:T(8,128)(2,1)} %param.12) | copy-start | bytes 786436
  15.9 10.7 %copy-start.4 = (bf16[256,512]{1,0:T(8,128)(2,1)S(1)}, bf16[256,512]{1,0:T(8,128)(2,1)}, u32[]{:S(2)}) copy-start(bf16[256,512]{1,0:T(8,128)(2,1)} %param.11) | copy-start | bytes 786436
  19.1 38.1 %all-to-all-start = ((f32[8,64,1024]{2,1,0:T(8,128)}), f32[8,64,1024]{2,1,0:T(8,128)}, u32[]{:S(2)}, u32[]{:S(2)}) async-start(f32[8,64,1024]{2,1,0:T(8,128)} %bitcast.155), calls=%async_computation | async-start | bytes 4194304 | tf_op jit(solution)/shard_map/all_to_all | solution.py:22
  26.6 79.8 %reduce-scatter.16.cloned.1.call-start = ((), (), s32[]{:S(2)}) async-start(), calls=%async_computation.20 | async-start | bytes 2359296 | tf_op jit(solution)/shard_map/reduce_scatter | solution.py:48
  95.1 32.8 %all-to-all-start.3 = ((f32[8,64,1024]{2,1,0:T(8,128)}), f32[8,64,1024]{2,1,0:T(8,128)}, u32[]{:S(2)}, u32[]{:S(2)}) async-start(f32[8,64,1024]{2,1,0:T(8,128)} %broadcast_in_dim.48), calls=%async_computation.3 | async-start | bytes 4194304 | tf_op jit(solution)/shard_map/all_to_all | solution.py:34
  99.5 129.9 %reduce-scatter.18.cloned.1.call-start = ((), (), s32[]{:S(2)}) async-start(), calls=%async_computation.21 | async-start | bytes 327680 | tf_op jit(solution)/shard_map/reduce_scatter | solution.py:48
  184.6 6.1 %copy-start.3 = (bf16[16,64,512]{2,1,0:T(8,128)(2,1)S(1)}, bf16[16,64,512]{2,1,0:T(8,128)(2,1)}, u32[]{:S(2)}) copy-start(bf16[16,64,512]{2,1,0:T(8,128)(2,1)} %fusion.19) | copy-start | bytes 3145732
  204.5 13.7 %all-to-all-start.8 = ((f32[2,2048,256]{2,1,0:T(8,128)}), f32[2,2048,256]{2,1,0:T(8,128)}, u32[]{:S(2)}, u32[]{:S(2)}) async-start(f32[2,2048,256]{2,1,0:T(8,128)} %bitcast.152), calls=%async_computation.8 | async-start | bytes 8388608 | tf_op jit(solution)/shard_map/all_to_all | solution.py:101
  218.2 35.6 %all-to-all-start.4 = ((f32[8,64,1024]{2,1,0:T(8,128)}), f32[8,64,1024]{2,1,0:T(8,128)}, u32[]{:S(2)}, u32[]{:S(2)}) async-start(f32[8,64,1024]{2,1,0:T(8,128)} %bitcast.153), calls=%async_computation.4 | async-start | bytes 4194304 | tf_op jit(solution)/shard_map/all_to_all | solution.py:22
  222.5 83.4 %reduce-scatter.20.cloned.1.call-start = ((), (), s32[]{:S(2)}) async-start(), calls=%async_computation.22 | async-start | bytes 98304 | tf_op jit(solution)/shard_map/reduce_scatter | solution.py:48
  229.4 77.3 %reduce-scatter.8.cloned.1.call-start = ((), (), s32[]{:S(2)}) async-start(), calls=%async_computation.16 | async-start | bytes 2359296 | tf_op jit(solution)/shard_map/reduce_scatter | solution.py:48
  255.5 39.1 %copy-start.2 = (bf16[256,16,64]{0,2,1:T(8,128)(2,1)S(1)}, bf16[256,16,64]{0,2,1:T(8,128)(2,1)}, u32[]{:S(2)}) copy-start(bf16[256,16,64]{0,2,1:T(8,128)(2,1)} %copy.57) | copy-start | bytes 1572868
  290.0 33.2 %all-to-all-start.7 = ((f32[8,64,1024]{2,1,0:T(8,128)}), f32[8,64,1024]{2,1,0:T(8,128)}, u32[]{:S(2)}, u32[]{:S(2)}) async-start(f32[8,64,1024]{2,1,0:T(8,128)} %broadcast_in_dim.50), calls=%async_computation.7 | async-start | bytes 4194304 | tf_op jit(solution)/shard_map/all_to_all | solution.py:34
  294.4 34.0 %reduce-scatter.10.cloned.1.call-start = ((), (), s32[]{:S(2)}) async-start(), calls=%async_computation.17 | async-start | bytes 327680 | tf_op jit(solution)/shard_map/reduce_scatter | solution.py:48
  306.8 40.4 %reduce-scatter.12.cloned.1.call-start = ((), (), s32[]{:S(2)}) async-start(), calls=%async_computation.18 | async-start | bytes 98304 | tf_op jit(solution)/shard_map/reduce_scatter | solution.py:48
  328.4 36.1 %reduce-scatter.14.cloned.1.call-start = ((), (), s32[]{:S(2)}) async-start(), calls=%async_computation.19 | async-start | bytes 49152 | tf_op jit(solution)/shard_map/reduce_scatter | solution.py:105
  365.3 5.8 %collective-permute-start = (f32[48,1024]{1,0:T(8,128)S(1)}, f32[48,1024]{1,0:T(8,128)}, u32[]{:S(2)}, u32[]{:S(2)}) collective-permute-start(f32[48,1024]{1,0:T(8,128)S(1)} %maximum_multiply_fusion), channel_id=1, source_target_pairs={{0,64},{64,0},{1,65},{65,1},{2,66},{66,2},{3,67},{67,3},{4,68},{68... | collective-permute-start | bytes 589832 | tf_op jit(solution)/shard_map/ppermute | solution.py:53
  372.1 6.6 %collective-permute-start.1 = (f32[48,1024]{1,0:T(8,128)S(1)}, f32[48,1024]{1,0:T(8,128)S(1)}, u32[]{:S(2)}, u32[]{:S(2)}) collective-permute-start(f32[48,1024]{1,0:T(8,128)S(1)} %fusion.49), channel_id=1, source_target_pairs={{0,128},{128,0},{1,129},{129,1},{2,130},{130,2},{3,131},{131,3},{4... | collective-permute-start | bytes 589832 | tf_op jit(solution)/shard_map/ppermute | solution.py:53
Sparse Core Ops, SparseCore 0:
  35.9 45.8 reduce-scatter.15
  106.5 25.4 reduce-scatter.17
  229.6 22.2 reduce-scatter.19
  254.4 40.9 reduce-scatter.7
  306.9 21.4 reduce-scatter.9
  330.7 16.4 reduce-scatter.11
  350.2 14.3 reduce-scatter.13

commit v2 on v1

v2 whole, which is shorter than its diff:
```python
import functools
import math

import jax
import jax.numpy as jnp
from jax import lax
from jax.experimental import pallas as pl
from jax.experimental.pallas import tpu as pltpu
from jax.sharding import Mesh
from jax.sharding import PartitionSpec as P

HEADS = 16
HEAD_DIM = 64
SPLITS = {64: (4, 8, 2), 8: (4, 2, 1)}
SEQ = ("x", "z", "yh")
VMEM_LIMIT = 40 * 1024 * 1024


def dot(a, b):
    return jnp.dot(a, b, preferred_element_type=jnp.float32)


def dot_t(a, b):
    return lax.dot_general(a, b, (((1,), (1,)), ((), ())), preferred_element_type=jnp.float32)


def project_kernel(x_ref, wq_ref, wk_ref, wv_ref, kproj_ref, vproj_ref, query_ref, part_ref, xt_ref, seen_ref):
    width = query_ref.shape[1]
    proj = kproj_ref.shape[0]
    x = x_ref[...]
    kproj, vproj = kproj_ref[...], vproj_ref[...]
    columns = pl.ds(pl.multiple_of(pl.program_id(0) * width, width), width)
    xt = x_ref[:, columns].T
    xt_ref[...] = xt
    n_z, _, chunk, _ = seen_ref.shape
    seen_ref[:, 0, :, :proj] = dot_t(xt, kproj).reshape(n_z, chunk, proj)
    seen_ref[:, 0, :, proj:] = dot_t(xt, vproj).reshape(n_z, chunk, proj)
    part_ref[:proj] = dot(kproj, dot(x, wk_ref[...]).astype(jnp.bfloat16))
    part_ref[proj:] = dot(vproj, dot(x, wv_ref[...]).astype(jnp.bfloat16))
    query_ref[...] = dot(x, wq_ref[...]).astype(jnp.bfloat16)


def project(inputs, w_query, w_key, w_value, key_proj, value_proj):
    rows, width = inputs.shape
    proj = key_proj.shape[0]
    n_x, n_z = lax.axis_size("x"), lax.axis_size("z")
    block = width // n_x
    whole = lambda a: pl.BlockSpec(a.shape, lambda i: (0, 0))
    weight = pl.BlockSpec((width, block), lambda i: (0, i))
    return pl.pallas_call(
        project_kernel,
        grid=(n_x,),
        in_specs=[whole(inputs), weight, weight, weight, whole(key_proj), whole(value_proj)],
        out_specs=[
            pl.BlockSpec((rows, block), lambda i: (0, i)),
            pl.BlockSpec((2 * proj, block), lambda i: (0, i)),
            pl.BlockSpec((block, rows), lambda i: (i, 0)),
            pl.BlockSpec((n_z, 1, block // n_z, 2 * proj), lambda i: (0, i, 0, 0)),
        ],
        out_shape=[
            jax.ShapeDtypeStruct((rows, width), jnp.bfloat16),
            jax.ShapeDtypeStruct((2 * proj, width), jnp.float32),
            jax.ShapeDtypeStruct((width, rows), jnp.bfloat16),
            jax.ShapeDtypeStruct((n_z, n_x, block // n_z, 2 * proj), jnp.float32),
        ],
        compiler_params=pltpu.CompilerParams(vmem_limit_bytes=VMEM_LIMIT),
        cost_estimate=pl.CostEstimate(
            flops=2 * rows * width * (3 * width + 4 * proj), bytes_accessed=14 << 20, transcendentals=0
        ),
        name="project",
    )(inputs, w_query, w_key, w_value, key_proj, value_proj)


def attend_kernel(
    norm, core_ref, q_ref, c_ref, ks_ref, vs_ref, xt_ref, att_ref, dq_ref, dsum_ref, other_ref, mine_ref
):
    step = pl.program_id(0)
    proj, block = ks_ref.shape
    scale = 1.0 / math.sqrt(HEAD_DIM)
    q, c = q_ref[...], c_ref[...]
    qt, ct = q.T, c.T
    kp = (ks_ref[...] * norm).astype(jnp.bfloat16).astype(jnp.float32)
    vp = (vs_ref[...] * norm).astype(jnp.bfloat16).astype(jnp.float32)
    kpt, vpt = kp.T, vp.T
    lane = lax.broadcasted_iota(jnp.int32, (proj, block), 1)
    sub = lax.broadcasted_iota(jnp.int32, (block, proj), 0)
    att = dq = dk = dv = None
    for h in range(block // HEAD_DIM):
        in_lane = (lane >= h * HEAD_DIM) & (lane < (h + 1) * HEAD_DIM)
        in_sub = (sub >= h * HEAD_DIM) & (sub < (h + 1) * HEAD_DIM)
        one = lambda mask, v: jnp.where(mask, v, 0.0).astype(jnp.bfloat16)
        scores = dot(one(in_lane, kp * scale), qt)
        top = jnp.max(scores, axis=0, keepdims=True)
        probs = jnp.exp(scores - top)
        probs = probs * (1.0 / jnp.sum(probs, axis=0, keepdims=True))
        low = probs.astype(jnp.bfloat16)
        dprob = dot(one(in_lane, vp), ct)
        delta = jnp.sum(probs * dprob, axis=0, keepdims=True)
        dscore = (probs * (dprob - delta)).astype(jnp.bfloat16)
        att_h = dot(one(in_sub, vpt), low)
        dq_h = dot(one(in_sub, kpt), dscore)
        dk_h = dot(dscore, q)
        dv_h = dot(low, c)
        if h == 0:
            att, dq, dk, dv = att_h, dq_h, dk_h, dv_h
        else:
            att, dq = att + att_h, dq + dq_h
            dk, dv = jnp.where(in_lane, dk_h, dk), jnp.where(in_lane, dv_h, dv)
    att_ref[...] = att.T.astype(jnp.bfloat16)
    dquery = (dq * scale).T.astype(jnp.bfloat16)
    dq_ref[...] = dquery
    dsum_ref[:proj] = dk * scale
    dsum_ref[proj:] = dv

    def put(ref):
        n_z, n_x, _, chunk, _ = ref.shape
        for x in range(n_x):
            rows = n_z * chunk
            term = dot(xt_ref[x * rows : (x + 1) * rows], dquery)
            ref[:, x, 0] = term.reshape(n_z, chunk, block)

    pl.when(step < 2)(functools.partial(put, other_ref))
    pl.when(step >= 2)(functools.partial(put, mine_ref))


def attend(query, cotangent, sums, inputs_t, norm):
    rows, width = query.shape
    proj = sums.shape[0] // 2
    n_x, n_z = lax.axis_size("x"), lax.axis_size("z")
    block = width // 4
    core = lax.axis_index("core").astype(jnp.int32).reshape(1)
    place = lambda i, core: lax.rem(i + 2 * (1 - core[0]), 4)
    tokens = pl.BlockSpec((rows, block), lambda i, core: (0, place(i, core)))
    terms = (n_z, n_x, 2, width // (n_x * n_z), block)
    terms_block = (n_z, n_x, 1, width // (n_x * n_z), block)
    return pl.pallas_call(
        functools.partial(attend_kernel, norm),
        grid_spec=pltpu.PrefetchScalarGridSpec(
            num_scalar_prefetch=1,
            grid=(4,),
            in_specs=[
                tokens,
                tokens,
                pl.BlockSpec((proj, block), lambda i, core: (0, place(i, core))),
                pl.BlockSpec((proj, block), lambda i, core: (1, place(i, core))),
                pl.BlockSpec((width, rows), lambda i, core: (0, 0)),
            ],
            out_specs=[
                tokens,
                tokens,
                pl.BlockSpec((2 * proj, block), lambda i, core: (0, place(i, core))),
                pl.BlockSpec(terms_block, lambda i, core: (0, 0, jnp.minimum(i, 1), 0, 0)),
                pl.BlockSpec(terms_block, lambda i, core: (0, 0, jnp.maximum(i - 2, 0), 0, 0)),
            ],
        ),
        out_shape=[
            jax.ShapeDtypeStruct((rows, width), jnp.bfloat16),
            jax.ShapeDtypeStruct((rows, width), jnp.bfloat16),
            jax.ShapeDtypeStruct((2 * proj, width), jnp.float32),
            jax.ShapeDtypeStruct(terms, jnp.float32),
            jax.ShapeDtypeStruct(terms, jnp.float32),
        ],
        compiler_params=pltpu.CompilerParams(vmem_limit_bytes=VMEM_LIMIT),
        cost_estimate=pl.CostEstimate(
            flops=8 * rows * width * proj * 6, bytes_accessed=12 << 20, transcendentals=rows * HEADS * proj
        ),
        name="attend",
    )(core, query, cotangent, sums, sums, inputs_t)


def scatter_sum(part):
    rows, width = part.shape
    plane = lax.axis_size(("x", "yh"))
    depth = lax.axis_size("z")
    got = lax.all_to_all(part.reshape(plane, rows // plane, width), ("x", "yh"), 0, 0)
    mine = jnp.sum(got, axis=0)
    got = lax.all_to_all(mine.reshape(depth, rows // plane // depth, width), "z", 0, 0)
    return jnp.sum(got, axis=0)


def gather_rows(mine):
    rows, width = mine.shape
    plane = lax.axis_size(("x", "yh"))
    depth = lax.axis_size("z")
    got = lax.all_to_all(jnp.broadcast_to(mine, (depth, rows, width)), "z", 0, 0)
    got = got.reshape(depth * rows, width)
    got = lax.all_to_all(jnp.broadcast_to(got, (plane, depth * rows, width)), ("x", "yh"), 0, 0)
    return got.reshape(plane * depth * rows, width)


def scatter_rows(part, axes):
    for axis in axes:
        part = lax.psum_scatter(part, axis, scatter_dimension=0, tiled=True)
    return part


def keep_half(part, axis):
    if lax.axis_size(axis) == 1:
        return part.reshape((-1,) + part.shape[2:])
    me = lax.axis_index(axis)
    other = lax.dynamic_index_in_dim(part, 1 - me, 0, keepdims=False)
    mine = lax.dynamic_index_in_dim(part, me, 0, keepdims=False)
    return mine + lax.ppermute(other, axis, [(0, 1), (1, 0)])


def pair_sum(part, axis):
    return part + lax.ppermute(part, axis, [(0, 1), (1, 0)])


def body(inputs, w_query, w_key, w_value, key_proj, value_proj, cotangent):
    inputs, cotangent = inputs[0], cotangent[0]
    rows, width = inputs.shape
    proj = key_proj.shape[0]
    n_seq = lax.axis_size(SEQ)
    n_data = lax.axis_size(("yl", "core"))
    norm = 1.0 / math.sqrt(rows * n_seq)
    factor = 1.0 / math.sqrt(rows * n_seq * n_data)

    query, part, inputs_t, seen = project(inputs, w_query, w_key, w_value, key_proj, value_proj)
    seen = scatter_rows(seen.reshape(width, 2 * proj), ("z", "x"))
    seen = keep_half(seen.reshape(2, -1, 2 * proj), "yh")
    sums = gather_rows(scatter_sum(part))

    attended, dquery, part, other, mine = attend(query, cotangent, sums, inputs_t, norm)

    grad_q = mine + lax.ppermute(other, "core", [(0, 1), (1, 0)])
    grad_q = scatter_rows(grad_q.reshape(-1, width // n_data), ("z", "x"))
    grad_q = keep_half(grad_q.reshape(2, -1, width // n_data), "yl")
    grad_q = keep_half(grad_q.reshape(2, -1, width // n_data), "yh")

    sums = gather_rows(scatter_sum(part))
    low = (sums * norm).astype(jnp.bfloat16)
    dkp_low, dvp_low = low[:proj], low[proj:]
    seen_high = seen.astype(jnp.bfloat16)
    seen_low = (seen - seen_high.astype(jnp.float32)).astype(jnp.bfloat16)
    grad_k = dot(seen_high[:, :proj], dkp_low) + dot(seen_low[:, :proj], dkp_low)
    grad_v = dot(seen_high[:, proj:], dvp_low) + dot(seen_low[:, proj:], dvp_low)
    place = lax.axis_index("core") * 2 + lax.axis_index("yl")
    column = lax.broadcasted_iota(jnp.int32, (1, n_data, 1), 1)
    grad_q = jnp.where(column == place, grad_q[:, None, :], 0.0).reshape(-1, width)
    grads = jnp.concatenate([grad_q, grad_k, grad_v], axis=0) * factor
    grads = pair_sum(pair_sum(grads, "core"), "yl")
    grad_q, grad_k, grad_v = jnp.split(grads, 3, axis=0)

    dkeys = lax.dot_general(
        key_proj, dkp_low, (((0,), (0,)), ((), ())), preferred_element_type=jnp.float32
    ).astype(jnp.bfloat16)
    dvalues = lax.dot_general(
        value_proj, dvp_low, (((0,), (0,)), ((), ())), preferred_element_type=jnp.float32
    ).astype(jnp.bfloat16)
    grad_in = dot_t(dquery, w_query)
    grad_in = grad_in + dot_t(dkeys, w_key)
    grad_in = grad_in + dot_t(dvalues, w_value)
    grad_inputs = grad_in.astype(jnp.bfloat16)
    return (attended[None], grad_inputs[None], grad_q, grad_k, grad_v)


def solution(mesh):
    split = SPLITS[mesh.shape["seq"]]
    fine = Mesh(mesh.devices.reshape((2, 2) + split), ("yl", "core") + SEQ)
    tokens = P(("yl", "core"), SEQ, None)
    return jax.shard_map(
        body,
        mesh=fine,
        in_specs=(tokens, P(), P(), P(), P(None, SEQ), P(None, SEQ), tokens),
        out_specs=(tokens, tokens, P(SEQ, None), P(SEQ, None), P(SEQ, None)),
        check_vma=False,
    )
```

time: 388 us -> 305 us (0.79)
  matrix products: 85.2 us -> 12.6 us
  Pallas kernels: 0 us -> 25.3 us
  local copies, waits for them, and re-layouts: 42.4 us -> 24.4 us
  other arithmetic: 25.8 us -> 8.87 us
  waiting for transfers between devices: 120 us -> 104 us
  blocking collectives: 66.5 us -> 81.7 us
    dot_general x20 -> x7, matrix products: 77.8 us -> 12.6 us  [the longest x3 11.9 us: dot_t(): lax.dot_general(a, b, (((1,), (1,)), ((), ())), preferred_element_type=jn...]
    all_to_all x0 -> x1, blocking collectives: none -> 33.8 us  [scatter_sum(): lax.all_to_all(part.reshape(plane, rows // plane, width), ('x', 'yh'), 0, 0)]
    pallas_call x0 -> x2, Pallas kernels: none -> 25.3 us  [the longest x1 15.1 us: attend(): pl.pallas_call(functools.partial(attend_kernel, norm), grid_spec=pltpu.Pr...]
    reduce_scatter x1 -> x0, waiting for transfers between devices: 15.8 us -> none  [body(): grad_q = lax.psum_scatter(grad_q, 'yl', scatter_dimension=0)]
    ppermute x0 -> x4, waiting for transfers between devices: none -> 14.9 us  [the longest x3 14.9 us: keep_half(): return mine + lax.ppermute(other, axis, [(0, 1), (1, 0)])]
    reshape x6 -> x0, local copies, waits for them, and re-layouts: 14.6 us -> none  [the longest x2 5.26 us: body(): key_h = low[:proj_rows].reshape(proj_rows, HEADS, head_dim)]
    unnamed x15 -> x45, local copies, waits for them, and re-layouts: 4.6 us -> 18.1 us
    all_to_all x2 -> x1, waiting for transfers between devices: 42.7 us -> 29.6 us  [scatter_sum(): lax.all_to_all(part.reshape(plane, rows // plane, width), ('x', 'yh'), 0, 0)]
  transfers between devices with their start and end apart: 14 -> 14, of which waited for: 9 -> 8; matrix products, arithmetic and copies ran while one was open for 36% -> 8% of each run, Pallas kernels for 0% -> 5%
where the time goes in v2:
time: 305 us; the launch traced here: 304 us
  waiting for transfers between devices  104 us (34%)
  blocking collectives  81.7 us (27%)
  starting transfers between devices  33.1 us (11%)
  Pallas kernels  25.3 us (8%)
  local copies, waits for them, and re-layouts  24.4 us (8%)
  between operations  14 us (5%)
  matrix products  12.6 us (4%)
  other arithmetic  8.87 us (3%)
    all_to_all x2, waiting for transfers between devices, gather_rows(): lax.all_to_all(jnp.broadcast_to(got, (plane, depth * rows, width)), ('x',...  34.9 us
    all_to_all x1, blocking collectives, scatter_sum(): lax.all_to_all(part.reshape(plane, rows // plane, width), ('x', 'yh'), 0, 0)  33.8 us
    all_to_all x2, blocking collectives, scatter_sum(): lax.all_to_all(mine.reshape(depth, rows // plane // depth, width), 'z', 0...  32.5 us
    all_to_all x1, waiting for transfers between devices, scatter_sum(): lax.all_to_all(part.reshape(plane, rows // plane, width), ('x', 'yh'), 0, 0)  29.6 us
    unnamed x45, local copies, waits for them, and re-layouts  18.1 us
    all_to_all x1, blocking collectives, gather_rows(): lax.all_to_all(jnp.broadcast_to(mine, (depth, rows, width)), 'z', 0, 0)  15.3 us
    pallas_call x1, Pallas kernels, attend(): pl.pallas_call(functools.partial(attend_kernel, norm), grid_spec=pltpu.Pr...  15.1 us
    ppermute x3, waiting for transfers between devices, keep_half(): return mine + lax.ppermute(other, axis, [(0, 1), (1, 0)])  14.9 us
  transfers between devices with their start and end apart: 14, of which 8 were waited for; matrix products, arithmetic and copies ran while one was open for 8% of the time, Pallas kernels for 5%

profile of v2, /device:TPU:1, one launch (start us, length us, event | category | flops | bytes accessed | tf_op | source)
XLA Modules:
  0.0 304.0 jit_solution(14737852845635121645)
XLA Ops:
  15.1 10.2 %project.1 = (bf16[512,1024]{1,0:T(8,128)(2,1)S(1)}, f32[512,1024]{1,0:T(8,128)S(1)}, bf16[1024,512]{1,0:T(8,128)(2,1)S(1)}, f32[8,4,32,512]{3,2,1,0:T(8,128)}) custom-call(bf16[512,1024]{1,0:T(8,128)(2,1)S(1)} %bitcast.55, bf16[1024,1024]{1,0:T(8,128)(2,1)S(1)} %copy-done.3, bf16[1024,1024]{1,0:T(8,128)(2,1)S(1)} %copy-done.5, ...), custom_call_target="tpu_custom_call" | custom-call | flops 4294967296 | bytes 14680064 | tf_op jit(solution)/shard_map/project/pallas_call | solution.py:50
  27.2 33.8 %all_to_all.40 = f32[8,64,1024]{2,1,0:T(8,128)S(1)} all-to-all(f32[8,64,1024]{2,1,0:T(8,128)S(1)} %bitcast.54), channel_id=1, replica_groups=mesh['yl'=2,'core'=2,'x'=4,'z'=8,'yh'=2] {'x','yh'}, dimensions={0} | all-to-all | bytes 4194304 | tf_op jit(solution)/shard_map/all_to_all | solution.py:175
  61.2 17.4 %all_to_all.41 = f32[8,8,1024]{2,1,0:T(8,128)S(1)} all-to-all(f32[8,8,1024]{2,1,0:T(8,128)S(1)} %bitcast.65), channel_id=1, replica_groups=mesh['yl'=2,'core'=2,'x'=4,'z'=8,'yh'=2] {'z'}, dimensions={0} | all-to-all | bytes 524288 | tf_op jit(solution)/shard_map/all_to_all | solution.py:177
  79.3 3.4 %all-to-all-start.2 = ((f32[8,8,1024]{2,1,0:T(8,128)}), f32[8,8,1024]{2,1,0:T(8,128)S(1)}, u32[]{:S(2)}, u32[]{:S(2)}) async-start(f32[8,8,1024]{2,1,0:T(8,128)} %broadcast_in_dim.45), calls=%async_computation.2 | async-start | bytes 524288 | tf_op jit(solution)/shard_map/all_to_all | solution.py:185
  83.5 8.6 %all-to-all-done.2 = f32[8,8,1024]{2,1,0:T(8,128)S(1)} async-done(((f32[8,8,1024]{2,1,0:T(8,128)}), f32[8,8,1024]{2,1,0:T(8,128)S(1)}, u32[]{:S(2)}, u32[]{:S(2)}) %all-to-all-start.2) | async-done | bytes 262176 | tf_op jit(solution)/shard_map/all_to_all | solution.py:185
  93.7 3.7 %all-to-all-start.3 = ((f32[8,64,1024]{2,1,0:T(8,128)}), f32[8,64,1024]{2,1,0:T(8,128)S(1)}, u32[]{:S(2)}, u32[]{:S(2)}) async-start(f32[8,64,1024]{2,1,0:T(8,128)} %broadcast_in_dim.46), calls=%async_computation.3 | async-start | bytes 4194304 | tf_op jit(solution)/shard_map/all_to_all | solution.py:187
  97.4 26.3 %all-to-all-done.3 = f32[8,64,1024]{2,1,0:T(8,128)S(1)} async-done(((f32[8,64,1024]{2,1,0:T(8,128)}), f32[8,64,1024]{2,1,0:T(8,128)S(1)}, u32[]{:S(2)}, u32[]{:S(2)}) %all-to-all-start.3) | async-done | bytes 2097184 | tf_op jit(solution)/shard_map/all_to_all | solution.py:187
  129.1 15.1 %attend.1 = (bf16[512,1024]{1,0:T(8,128)(2,1)}, bf16[512,1024]{1,0:T(8,128)(2,1)S(1)}, f32[512,1024]{1,0:T(8,128)S(1)}, f32[8,4,2,32,256]{4,3,2,1,0:T(8,128)}, f32[8,4,2,32,256]{4,3,2,1,0:T(8,128)S(1)}) custom-call(s32[1]{0:T(128)} %bitcast.core_ref, bf16[512,1024]{1,0:T(8,128)(2,1)S(1)} %copy-done.17, bf16[512,1024]{1,0:T(8,128)(2,1)S(1)} %bitcast.56, ...), custom_call_target="tpu_custom_call" | custom-call | flops 6442450944 | bytes 12582912 | tf_op jit(solution)/shard_map/attend/pallas_call | solution.py:136
  146.5 3.5 %collective-permute-start = (f32[8,4,2,32,256]{4,3,2,1,0:T(8,128)}, f32[8,4,2,32,256]{4,3,2,1,0:T(8,128)}, u32[]{:S(2)}, u32[]{:S(2)}) collective-permute-start(f32[8,4,2,32,256]{4,3,2,1,0:T(8,128)} %get-tuple-element.21), channel_id=1, source_target_pairs={{0,64},{64,0},{1,65},{65,1},{2,66},{66,2},{3,67},{67,3},{4,68},{68... | collective-permute-start | bytes 6291464 | tf_op jit(solution)/shard_map/ppermute | solution.py:226
  150.0 4.3 %all-to-all-start.4 = ((f32[8,64,1024]{2,1,0:T(8,128)}), f32[8,64,1024]{2,1,0:T(8,128)}, u32[]{:S(2)}, u32[]{:S(2)}) async-start(f32[8,64,1024]{2,1,0:T(8,128)} %bitcast.51), calls=%async_computation.4 | async-start | bytes 4194304 | tf_op jit(solution)/shard_map/all_to_all | solution.py:175
  155.2 3.3 %add.63 = f32[8,4,2,32,256]{4,3,2,1,0:T(8,128)} add(f32[8,4,2,32,256]{4,3,2,1,0:T(8,128)S(1)} %get-tuple-element.20, f32[8,4,2,32,256]{4,3,2,1,0:T(8,128)} %collective-permute-done) | non-fusion elementwise | flops 524288 | bytes 6291456 | tf_op jit(solution)/shard_map/add | solution.py:226
  158.5 29.6 %all-to-all-done.4 = f32[8,64,1024]{2,1,0:T(8,128)} async-done(((f32[8,64,1024]{2,1,0:T(8,128)}), f32[8,64,1024]{2,1,0:T(8,128)}, u32[]{:S(2)}, u32[]{:S(2)}) %all-to-all-start.4) | async-done | bytes 2097184 | tf_op jit(solution)/shard_map/all_to_all | solution.py:175
  189.8 15.1 %all_to_all.42 = f32[8,8,1024]{2,1,0:T(8,128)S(1)} all-to-all(f32[8,8,1024]{2,1,0:T(8,128)S(1)} %bitcast.66), channel_id=1, replica_groups=mesh['yl'=2,'core'=2,'x'=4,'z'=8,'yh'=2] {'z'}, dimensions={0} | all-to-all | bytes 524288 | tf_op jit(solution)/shard_map/all_to_all | solution.py:177
  205.0 15.3 %all_to_all.43 = f32[8,8,1024]{2,1,0:T(8,128)S(1)} all-to-all(f32[8,8,1024]{2,1,0:T(8,128)S(1)} %broadcast_in_dim.48), channel_id=1, replica_groups=mesh['yl'=2,'core'=2,'x'=4,'z'=8,'yh'=2] {'z'}, dimensions={0} | all-to-all | bytes 524288 | tf_op jit(solution)/shard_map/all_to_all | solution.py:185
  222.0 4.6 %all-to-all-start.7 = ((f32[8,64,1024]{2,1,0:T(8,128)}), f32[8,64,1024]{2,1,0:T(8,128)}, u32[]{:S(2)}, u32[]{:S(2)}) async-start(f32[8,64,1024]{2,1,0:T(8,128)} %broadcast_in_dim.49), calls=%async_computation.7 | async-start | bytes 4194304 | tf_op jit(solution)/shard_map/all_to_all | solution.py:187
  227.5 2.8 collective-permute-start.3
  230.3 2.6 fusion.13
  232.9 12.4 %collective-permute-done.3 = f32[16,512]{1,0:T(8,128)S(1)} collective-permute-done((f32[16,512]{1,0:T(8,128)S(1)}, f32[16,512]{1,0:T(8,128)S(1)}, u32[]{:S(2)}, u32[]{:S(2)}) %collective-permute-start.3) | collective-permute-done | bytes 32800 | tf_op jit(solution)/shard_map/ppermute | solution.py:203
  245.3 8.5 %all-to-all-done.7 = f32[8,64,1024]{2,1,0:T(8,128)} async-done(((f32[8,64,1024]{2,1,0:T(8,128)}), f32[8,64,1024]{2,1,0:T(8,128)}, u32[]{:S(2)}, u32[]{:S(2)}) %all-to-all-start.7) | async-done | bytes 2097184 | tf_op jit(solution)/shard_map/all_to_all | solution.py:187
  256.8 14.5 %reduce-scatter.7.cloned.1.call-done = f32[64,256]{1,0:T(8,128)} async-done(((f32[256,256]{1,0:T(8,128)}), f32[64,256]{1,0:T(8,128)}) %reduce-scatter.7.cloned.1.call-update) | async-done | bytes 65552 | tf_op jit(solution)/shard_map/reduce_scatter | solution.py:193
  275.6 2.8 collective-permute-start.2
  279.9 5.3 %collective-permute-start.4 = (f32[48,1024]{1,0:T(8,128)S(1)}, f32[48,1024]{1,0:T(8,128)}, u32[]{:S(2)}, u32[]{:S(2)}) collective-permute-start(f32[48,1024]{1,0:T(8,128)S(1)} %maximum_multiply_fusion), channel_id=1, source_target_pairs={{0,64},{64,0},{1,65},{65,1},{2,66},{66,2},{3,67},{67,3},{4,68},{68... | collective-permute-start | bytes 589832 | tf_op jit(solution)/shard_map/ppermute | solution.py:207
  285.2 3.9 %fusion.1 = f32[512,1024]{1,0:T(8,128)} fusion(bf16[1024,1024]{1,0:T(8,128)(2,1)S(1)} %copy-done.6, bf16[256,1024]{1,0:T(8,128)(2,1)} %bitcast.63, bf16[256,512]{1,0:T(8,128)(2,1)S(1)} %copy-done.11), kind=kOutput, calls=%fused_computation.5 | convolution fusion | flops 1342701568 | bytes 4980736 | tf_op jit(solution)/shard_map/dot_general | solution.py:24
  291.4 5.4 %fusion = bf16[1,512,1024]{2,1,0:T(8,128)(2,1)} fusion(bf16[1024,1024]{1,0:T(8,128)(2,1)} %wv_ref.1, f32[512,1024]{1,0:T(8,128)} %fusion.13, f32[512,1024]{1,0:T(8,128)} %fusion.1, bf16[256,1024]{1,0:T(8,128)(2,1)S(1)} %bitcast.60, bf16[256,512]{1,0:T(8,128)(2,1)S(1)} %copy-done.13), kind=kOutput, calls=%fused_computation.4 | convolution fusion | flops 1344274432 | bytes 8126464 | tf_op jit(solution)/shard_map/dot_general | solution.py:24
  (92 shorter events, 37.4 us)
Async XLA Ops:
  7.2 1.6 copy-start.3
  8.8 1.6 copy-start.5
  79.3 12.8 %all-to-all-start.2 = ((f32[8,8,1024]{2,1,0:T(8,128)}), f32[8,8,1024]{2,1,0:T(8,128)S(1)}, u32[]{:S(2)}, u32[]{:S(2)}) async-start(f32[8,8,1024]{2,1,0:T(8,128)} %broadcast_in_dim.45), calls=%async_computation.2 | async-start | bytes 524288 | tf_op jit(solution)/shard_map/all_to_all | solution.py:185
  82.7 71.7 %reduce-scatter.9.cloned.1.call-start = ((), (), s32[]{:S(2)}) async-start(), calls=%async_computation.14 | async-start | bytes 2359296 | tf_op jit(solution)/shard_map/reduce_scatter | solution.py:193
  93.7 31.4 %copy-start.9 = (bf16[1,512,1024]{2,1,0:T(8,128)(2,1)S(1)}, bf16[1,512,1024]{2,1,0:T(8,128)(2,1)}, u32[]{:S(2)}) copy-start(bf16[1,512,1024]{2,1,0:T(8,128)(2,1)} %param.13) | copy-start | bytes 3145732
  93.7 30.1 %all-to-all-start.3 = ((f32[8,64,1024]{2,1,0:T(8,128)}), f32[8,64,1024]{2,1,0:T(8,128)S(1)}, u32[]{:S(2)}, u32[]{:S(2)}) async-start(f32[8,64,1024]{2,1,0:T(8,128)} %broadcast_in_dim.46), calls=%async_computation.3 | async-start | bytes 4194304 | tf_op jit(solution)/shard_map/all_to_all | solution.py:187
  125.0 1.6 copy-start.2
  146.5 8.7 %collective-permute-start = (f32[8,4,2,32,256]{4,3,2,1,0:T(8,128)}, f32[8,4,2,32,256]{4,3,2,1,0:T(8,128)}, u32[]{:S(2)}, u32[]{:S(2)}) collective-permute-start(f32[8,4,2,32,256]{4,3,2,1,0:T(8,128)} %get-tuple-element.21), channel_id=1, source_target_pairs={{0,64},{64,0},{1,65},{65,1},{2,66},{66,2},{3,67},{67,3},{4,68},{68... | collective-permute-start | bytes 6291464 | tf_op jit(solution)/shard_map/ppermute | solution.py:226
  150.0 38.1 %all-to-all-start.4 = ((f32[8,64,1024]{2,1,0:T(8,128)}), f32[8,64,1024]{2,1,0:T(8,128)}, u32[]{:S(2)}, u32[]{:S(2)}) async-start(f32[8,64,1024]{2,1,0:T(8,128)} %bitcast.51), calls=%async_computation.4 | async-start | bytes 4194304 | tf_op jit(solution)/shard_map/all_to_all | solution.py:175
  154.4 72.4 %reduce-scatter.11.cloned.1.call-start = ((), (), s32[]{:S(2)}) async-start(), calls=%async_computation.15 | async-start | bytes 327680 | tf_op jit(solution)/shard_map/reduce_scatter | solution.py:193
  155.1 100.6 %reduce-scatter.5.cloned.1.call-start = ((), (), s32[]{:S(2)}) async-start(), calls=%async_computation.12 | async-start | bytes 2359296 | tf_op jit(solution)/shard_map/reduce_scatter | solution.py:193
  222.0 8.3 %copy-start.4 = (bf16[1024,1024]{1,0:T(8,128)(2,1)S(1)}, bf16[1024,1024]{1,0:T(8,128)(2,1)}, u32[]{:S(2)}) copy-start(bf16[1024,1024]{1,0:T(8,128)(2,1)} %wq_ref.1) | copy-start | bytes 6291460
  222.0 8.3 %copy-start.15 = (bf16[512,1024]{1,0:T(8,128)(2,1)S(1)}, bf16[512,1024]{1,0:T(8,128)(2,1)}, u32[]{:S(2)}) copy-start(bf16[512,1024]{1,0:T(8,128)(2,1)} %copy-done.14) | copy-start | bytes 3145732
  222.0 31.8 %all-to-all-start.7 = ((f32[8,64,1024]{2,1,0:T(8,128)}), f32[8,64,1024]{2,1,0:T(8,128)}, u32[]{:S(2)}, u32[]{:S(2)}) async-start(f32[8,64,1024]{2,1,0:T(8,128)} %broadcast_in_dim.49), calls=%async_computation.7 | async-start | bytes 4194304 | tf_op jit(solution)/shard_map/all_to_all | solution.py:187
  226.6 44.7 %reduce-scatter.7.cloned.1.call-start = ((), (), s32[]{:S(2)}) async-start(), calls=%async_computation.13 | async-start | bytes 327680 | tf_op jit(solution)/shard_map/reduce_scatter | solution.py:193
  227.5 17.7 %collective-permute-start.3 = (f32[16,512]{1,0:T(8,128)S(1)}, f32[16,512]{1,0:T(8,128)S(1)}, u32[]{:S(2)}, u32[]{:S(2)}) collective-permute-start(f32[16,512]{1,0:T(8,128)S(1)} %dynamic-slice_bitcast_fusion), channel_id=1, source_target_pairs={{0,1},{1,0},{2,3},{3,2},{4,5},{5,4},{6,7},{7,6},{8,9},{9,8},{10,11... | collective-permute-start | bytes 98312 | tf_op jit(solution)/shard_map/ppermute | solution.py:203
  230.3 15.0 %copy-start.21 = (f32[32,512]{1,0:T(8,128)S(1)}, f32[32,512]{1,0:T(8,128)}, u32[]{:S(2)}) copy-start(f32[32,512]{1,0:T(8,128)} %reduce-scatter.11.cloned.1.call-done) | copy-start | bytes 196612
  255.8 29.3 %copy-start.6 = (bf16[1024,1024]{1,0:T(8,128)(2,1)S(1)}, bf16[1024,1024]{1,0:T(8,128)(2,1)}, u32[]{:S(2)}) copy-start(bf16[1024,1024]{1,0:T(8,128)(2,1)} %wk_ref.1) | copy-start | bytes 6291460
  255.8 29.3 %copy-start.11 = (bf16[256,512]{1,0:T(8,128)(2,1)S(1)}, bf16[256,512]{1,0:T(8,128)(2,1)}, u32[]{:S(2)}) copy-start(bf16[256,512]{1,0:T(8,128)(2,1)} %kproj_ref.1) | copy-start | bytes 786436
  272.1 2.8 collective-permute-start.1
  275.6 4.1 %collective-permute-start.2 = (f32[16,256]{1,0:T(8,128)S(1)}, f32[16,256]{1,0:T(8,128)S(1)}, u32[]{:S(2)}, u32[]{:S(2)}) collective-permute-start(f32[16,256]{1,0:T(8,128)S(1)} %dynamic-slice_bitcast_fusion.2), channel_id=1, source_target_pairs={{0,1},{1,0},{2,3},{3,2},{4,5},{5,4},{6,7},{7,6},{8,9},{9,8},{10,11... | collective-permute-start | bytes 49160 | tf_op jit(solution)/shard_map/ppermute | solution.py:203
  279.9 11.5 %copy-start.13 = (bf16[256,512]{1,0:T(8,128)(2,1)S(1)}, bf16[256,512]{1,0:T(8,128)(2,1)}, u32[]{:S(2)}) copy-start(bf16[256,512]{1,0:T(8,128)(2,1)} %vproj_ref.1) | copy-start | bytes 786436
  279.9 9.2 %collective-permute-start.4 = (f32[48,1024]{1,0:T(8,128)S(1)}, f32[48,1024]{1,0:T(8,128)}, u32[]{:S(2)}, u32[]{:S(2)}) collective-permute-start(f32[48,1024]{1,0:T(8,128)S(1)} %maximum_multiply_fusion), channel_id=1, source_target_pairs={{0,64},{64,0},{1,65},{65,1},{2,66},{66,2},{3,67},{67,3},{4,68},{68... | collective-permute-start | bytes 589832 | tf_op jit(solution)/shard_map/ppermute | solution.py:207
  290.1 6.7 %collective-permute-start.5 = (f32[48,1024]{1,0:T(8,128)S(1)}, f32[48,1024]{1,0:T(8,128)S(1)}, u32[]{:S(2)}, u32[]{:S(2)}) collective-permute-start(f32[48,1024]{1,0:T(8,128)S(1)} %fusion.9), channel_id=1, source_target_pairs={{0,128},{128,0},{1,129},{129,1},{2,130},{130,2},{3,131},{131,3},{4... | collective-permute-start | bytes 589832 | tf_op jit(solution)/shard_map/ppermute | solution.py:207
  (12 other events, 13.5 us)
Sparse Core Ops, SparseCore 0:
  86.1 39.4 reduce-scatter.8
  157.7 18.2 reduce-scatter.10
  178.8 50.3 reduce-scatter.4
  255.9 15.4 reduce-scatter.6

commit v3 on v2

--- a/solution.py
+++ b/solution.py
@@ -11,9 +11,11 @@
 
 HEADS = 16
 HEAD_DIM = 64
-SPLITS = {64: (4, 8, 2), 8: (4, 2, 1)}
-SEQ = ("x", "z", "yh")
-VMEM_LIMIT = 40 * 1024 * 1024
+SPLITS = {64: (4, 4, 2, 2), 8: (4, 2, 1, 1)}
+SEQ = ("x", "zh", "zl", "yh")
+Z = ("zh", "zl")
+NEAR = ("x", "zl", "yh")
+VMEM_LIMIT = 60 * 1024 * 1024
 
 
 def dot(a, b):
@@ -43,7 +45,7 @@
 def project(inputs, w_query, w_key, w_value, key_proj, value_proj):
     rows, width = inputs.shape
     proj = key_proj.shape[0]
-    n_x, n_z = lax.axis_size("x"), lax.axis_size("z")
+    n_x, n_z = lax.axis_size("x"), lax.axis_size(Z)
     block = width // n_x
     whole = lambda a: pl.BlockSpec(a.shape, lambda i: (0, 0))
     weight = pl.BlockSpec((width, block), lambda i: (0, i))
@@ -126,7 +128,7 @@
 def attend(query, cotangent, sums, inputs_t, norm):
     rows, width = query.shape
     proj = sums.shape[0] // 2
-    n_x, n_z = lax.axis_size("x"), lax.axis_size("z")
+    n_x, n_z = lax.axis_size("x"), lax.axis_size(Z)
     block = width // 4
     core = lax.axis_index("core").astype(jnp.int32).reshape(1)
     place = lambda i, core: lax.rem(i + 2 * (1 - core[0]), 4)
@@ -168,35 +170,69 @@
     )(core, query, cotangent, sums, sums, inputs_t)
 
 
+def input_grads_kernel(
+    norm, sums_ref, dq_ref, kproj_ref, vproj_ref, wq_ref, wk_ref, wv_ref, out_ref, dkeys_ref, dvalues_ref
+):
+    proj = kproj_ref.shape[0]
+
+    @pl.when(pl.program_id(0) == 0)
+    def _():
+        dkp = (sums_ref[:proj] * norm).astype(jnp.bfloat16)
+        dkeys_ref[...] = dot(kproj_ref[...].T, dkp).astype(jnp.bfloat16)
+        dvp = (sums_ref[proj:] * norm).astype(jnp.bfloat16)
+        dvalues_ref[...] = dot(vproj_ref[...].T, dvp).astype(jnp.bfloat16)
+
+    grad = dot_t(dq_ref[...], wq_ref[...]) + dot_t(dkeys_ref[...], wk_ref[...])
+    out_ref[...] = (grad + dot_t(dvalues_ref[...], wv_ref[...])).astype(jnp.bfloat16)
+
+
+def input_grads(sums, dquery, key_proj, value_proj, w_query, w_key, w_value, norm):
+    rows, width = dquery.shape
+    block = width // 4
+    whole = lambda a: pl.BlockSpec(a.shape, lambda i: (0, 0))
+    weight = pl.BlockSpec((block, width), lambda i: (i, 0))
+    return pl.pallas_call(
+        functools.partial(input_grads_kernel, norm),
+        grid=(4,),
+        in_specs=[whole(sums), whole(dquery), whole(key_proj), whole(value_proj), weight, weight, weight],
+        out_specs=pl.BlockSpec((rows, block), lambda i: (0, i)),
+        out_shape=jax.ShapeDtypeStruct((rows, width), jnp.bfloat16),
+        scratch_shapes=[pltpu.VMEM((rows, width), jnp.bfloat16)] * 2,
+        compiler_params=pltpu.CompilerParams(vmem_limit_bytes=VMEM_LIMIT),
+        cost_estimate=pl.CostEstimate(
+            flops=2 * rows * width * (3 * width + sums.shape[0]), bytes_accessed=11 << 20, transcendentals=0
+        ),
+        name="input_grads",
+    )(sums, dquery, key_proj, value_proj, w_query, w_key, w_value)
+
+
 def scatter_sum(part):
     rows, width = part.shape
-    plane = lax.axis_size(("x", "yh"))
-    depth = lax.axis_size("z")
-    got = lax.all_to_all(part.reshape(plane, rows // plane, width), ("x", "yh"), 0, 0)
+    plane = lax.axis_size(NEAR)
+    depth = lax.axis_size("zh")
+    got = lax.all_to_all(part.reshape(plane, rows // plane, width), NEAR, 0, 0)
     mine = jnp.sum(got, axis=0)
-    got = lax.all_to_all(mine.reshape(depth, rows // plane // depth, width), "z", 0, 0)
+    got = lax.all_to_all(mine.reshape(depth, rows // plane // depth, width), "zh", 0, 0)
     return jnp.sum(got, axis=0)
 
 
-def gather_rows(mine):
+def gather_rows(mine, beside):
     rows, width = mine.shape
-    plane = lax.axis_size(("x", "yh"))
-    depth = lax.axis_size("z")
-    got = lax.all_to_all(jnp.broadcast_to(mine, (depth, rows, width)), "z", 0, 0)
-    got = got.reshape(depth * rows, width)
-    got = lax.all_to_all(jnp.broadcast_to(got, (plane, depth * rows, width)), ("x", "yh"), 0, 0)
-    return got.reshape(plane * depth * rows, width)
-
-
-def scatter_rows(part, axes):
-    for axis in axes:
-        part = lax.psum_scatter(part, axis, scatter_dimension=0, tiled=True)
-    return part
+    plane = lax.axis_size(NEAR)
+    depth = lax.axis_size("zh")
+    got = lax.all_to_all(jnp.broadcast_to(mine, (depth, rows, width)), "zh", 0, 0)
+    got, beside = lax.optimization_barrier((got.reshape(depth * rows, width), beside))
+    got = lax.all_to_all(jnp.broadcast_to(got, (plane, depth * rows, width)), NEAR, 0, 0)
+    return got.reshape(plane * depth * rows, width), beside
+
+
+def scatter_rows(part, axis):
+    return lax.psum_scatter(part, axis, scatter_dimension=0, tiled=True)
 
 
 def keep_half(part, axis):
     if lax.axis_size(axis) == 1:
-        return part.reshape((-1,) + part.shape[2:])
+        return part[0]
     me = lax.axis_index(axis)
     other = lax.dynamic_index_in_dim(part, 1 - me, 0, keepdims=False)
     mine = lax.dynamic_index_in_dim(part, me, 0, keepdims=False)
@@ -212,46 +248,42 @@
     rows, width = inputs.shape
     proj = key_proj.shape[0]
     n_seq = lax.axis_size(SEQ)
+    n_yh = lax.axis_size("yh")
     n_data = lax.axis_size(("yl", "core"))
     norm = 1.0 / math.sqrt(rows * n_seq)
     factor = 1.0 / math.sqrt(rows * n_seq * n_data)
 
     query, part, inputs_t, seen = project(inputs, w_query, w_key, w_value, key_proj, value_proj)
-    seen = scatter_rows(seen.reshape(width, 2 * proj), ("z", "x"))
-    seen = keep_half(seen.reshape(2, -1, 2 * proj), "yh")
-    sums = gather_rows(scatter_sum(part))
+    seen = scatter_rows(seen.reshape(width, 2 * proj), Z)
+    sums, seen = gather_rows(scatter_sum(part), seen)
+    sums, seen = lax.optimization_barrier((sums, scatter_rows(seen, "x")))
+    seen = keep_half(seen.reshape(n_yh, -1, 2 * proj), "yh")
 
     attended, dquery, part, other, mine = attend(query, cotangent, sums, inputs_t, norm)
 
+    part, seen = lax.optimization_barrier((part, seen))
+
     grad_q = mine + lax.ppermute(other, "core", [(0, 1), (1, 0)])
-    grad_q = scatter_rows(grad_q.reshape(-1, width // n_data), ("z", "x"))
-    grad_q = keep_half(grad_q.reshape(2, -1, width // n_data), "yl")
-    grad_q = keep_half(grad_q.reshape(2, -1, width // n_data), "yh")
-
-    sums = gather_rows(scatter_sum(part))
+    grad_q = scatter_rows(grad_q.reshape(-1, width // n_data), Z)
+    sums, grad_q = gather_rows(scatter_sum(part), grad_q)
+    sums, grad_q = lax.optimization_barrier((sums, scatter_rows(grad_q, "x")))
+    grad_q = jnp.moveaxis(grad_q.reshape(2, n_yh, -1, width // n_data), 1, 0)
+    grad_q = keep_half(grad_q, "yh")
+    grad_q = jnp.concatenate([grad_q[0], grad_q[1]], axis=1)
+
     low = (sums * norm).astype(jnp.bfloat16)
     dkp_low, dvp_low = low[:proj], low[proj:]
     seen_high = seen.astype(jnp.bfloat16)
     seen_low = (seen - seen_high.astype(jnp.float32)).astype(jnp.bfloat16)
     grad_k = dot(seen_high[:, :proj], dkp_low) + dot(seen_low[:, :proj], dkp_low)
     grad_v = dot(seen_high[:, proj:], dvp_low) + dot(seen_low[:, proj:], dvp_low)
-    place = lax.axis_index("core") * 2 + lax.axis_index("yl")
-    column = lax.broadcasted_iota(jnp.int32, (1, n_data, 1), 1)
-    grad_q = jnp.where(column == place, grad_q[:, None, :], 0.0).reshape(-1, width)
+    core = lax.axis_index("core")
+    grad_q = jnp.concatenate([jnp.where(core == i, grad_q, 0.0) for i in range(2)], axis=1)
     grads = jnp.concatenate([grad_q, grad_k, grad_v], axis=0) * factor
     grads = pair_sum(pair_sum(grads, "core"), "yl")
     grad_q, grad_k, grad_v = jnp.split(grads, 3, axis=0)
 
-    dkeys = lax.dot_general(
-        key_proj, dkp_low, (((0,), (0,)), ((), ())), preferred_element_type=jnp.float32
-    ).astype(jnp.bfloat16)
-    dvalues = lax.dot_general(
-        value_proj, dvp_low, (((0,), (0,)), ((), ())), preferred_element_type=jnp.float32
-    ).astype(jnp.bfloat16)
-    grad_in = dot_t(dquery, w_query)
-    grad_in = grad_in + dot_t(dkeys, w_key)
-    grad_in = grad_in + dot_t(dvalues, w_value)
-    grad_inputs = grad_in.astype(jnp.bfloat16)
+    grad_inputs = input_grads(sums, dquery, key_proj, value_proj, w_query, w_key, w_value, norm)
     return (attended[None], grad_inputs[None], grad_q, grad_k, grad_v)
 
 

time: 305 us -> 278 us (0.911)
  blocking collectives: 81.7 us -> 37.3 us
  waiting for transfers between devices: 104 us -> 137 us
  local copies, waits for them, and re-layouts: 24.4 us -> 6.57 us
  matrix products: 12.6 us -> 0.74 us
  Pallas kernels: 25.3 us -> 36.8 us
  starting transfers between devices: 33.1 us -> 39.8 us
  other arithmetic: 8.87 us -> 4.73 us
    reduce_scatter x4, waiting for transfers between devices: 14.6 us -> 64.1 us  [scatter_rows(): return lax.psum_scatter(part, axis, scatter_dimension=0, tiled=True)]
    all_to_all x4 -> x3, blocking collectives: 81.7 us -> 37.3 us  [the longest x2 27.3 us: scatter_sum(): lax.all_to_all(mine.reshape(depth, rows // plane // depth, width), 'zh',...]
    unnamed x45 -> x8, local copies, waits for them, and re-layouts: 18.1 us -> 2.04 us
    all_to_all x4 -> x5, starting transfers between devices: 16.1 us -> 29.2 us  [the longest x2 16.8 us: scatter_sum(): got = lax.all_to_all(part.reshape(plane, rows // plane, width), NEAR, 0, 0)]
    ppermute x3 -> x2, waiting for transfers between devices: 14.9 us -> 2.71 us  [keep_half(): return mine + lax.ppermute(other, axis, [(0, 1), (1, 0)])]
    dot_general x3 -> x0, matrix products: 11.9 us -> none  [dot_t(): lax.dot_general(a, b, (((1,), (1,)), ((), ())), preferred_element_type=jn...]
    pallas_call x0 -> x1, Pallas kernels: none -> 8.7 us  [input_grads(): pl.pallas_call(functools.partial(input_grads_kernel, norm), grid=(4,), in...]
    all_to_all x4 -> x5, waiting for transfers between devices: 73.1 us -> 67.7 us  [the longest x2 60.5 us: scatter_sum(): got = lax.all_to_all(part.reshape(plane, rows // plane, width), NEAR, 0, 0)]
  transfers between devices with their start and end apart: 14 -> 14, of which waited for: 8 -> 8; matrix products, arithmetic and copies ran while one was open for 8% -> 2% of each run, Pallas kernels for 5% -> 3%
where the time goes in v3:
time: 278 us; the launch traced here: 277 us
  waiting for transfers between devices  137 us (49%)
  starting transfers between devices  39.8 us (14%)
  blocking collectives  37.3 us (13%)
  Pallas kernels  36.8 us (13%)
  between operations  13.9 us (5%)
  local copies, waits for them, and re-layouts  6.57 us (2%)
  other arithmetic  4.73 us (2%)
    reduce_scatter x4, waiting for transfers between devices, scatter_rows(): return lax.psum_scatter(part, axis, scatter_dimension=0, tiled=True)  64.1 us
    all_to_all x2, waiting for transfers between devices, scatter_sum(): got = lax.all_to_all(part.reshape(plane, rows // plane, width), NEAR, 0, 0)  60.5 us
    all_to_all x2, blocking collectives, scatter_sum(): lax.all_to_all(mine.reshape(depth, rows // plane // depth, width), 'zh',...  27.3 us
    all_to_all x2, starting transfers between devices, scatter_sum(): got = lax.all_to_all(part.reshape(plane, rows // plane, width), NEAR, 0, 0)  16.8 us
    pallas_call x1, Pallas kernels, attend(): pl.pallas_call(functools.partial(attend_kernel, norm), grid_spec=pltpu.Pr...  16.7 us
    pallas_call x1, Pallas kernels, project(): pl.pallas_call(project_kernel, grid=(n_x,), in_specs=[whole(inputs), weig...  11.4 us
    all_to_all x1, blocking collectives, gather_rows(): lax.all_to_all(jnp.broadcast_to(mine, (depth, rows, width)), 'zh', 0, 0)  10.1 us
    all_to_all x2, starting transfers between devices, gather_rows(): lax.all_to_all(jnp.broadcast_to(got, (plane, depth * rows, width)), NEAR,...  9.07 us
  transfers between devices with their start and end apart: 14, of which 8 were waited for; matrix products, arithmetic and copies ran while one was open for 2% of the time, Pallas kernels for 3%

profile of v3, /device:TPU:1, one launch (start us, length us, event | category | flops | bytes accessed | tf_op | source)
XLA Modules:
  0.0 277.3 jit_solution(11872027228086552626)
XLA Ops:
  7.2 11.4 %project.1 = (bf16[512,1024]{1,0:T(8,128)(2,1)}, f32[512,1024]{1,0:T(8,128)}, bf16[1024,512]{1,0:T(8,128)(2,1)}, f32[8,4,32,512]{3,2,1,0:T(8,128)}) custom-call(bf16[512,1024]{1,0:T(8,128)(2,1)} %bitcast.49, bf16[1024,1024]{1,0:T(8,128)(2,1)} %wq_ref.3, bf16[1024,1024]{1,0:T(8,128)(2,1)} %wk_ref.3, bf16[1024,1024]{1,0:T(8,128)(2,1)} %wv_ref.3, ...), custom_call_target="tpu_custom_call" | custom-call | flops 4294967296 | bytes 14680064 | tf_op jit(solution)/shard_map/project/pallas_call | solution.py:52
  18.5 8.9 %all-to-all-start = ((f32[16,32,1024]{2,1,0:T(8,128)}), f32[16,32,1024]{2,1,0:T(8,128)S(1)}, u32[]{:S(2)}, u32[]{:S(2)}) async-start(f32[16,32,1024]{2,1,0:T(8,128)} %bitcast.40), calls=%async_computation | async-start | bytes 4194304 | tf_op jit(solution)/shard_map/all_to_all | solution.py:213
  28.2 32.3 %all-to-all-done = f32[16,32,1024]{2,1,0:T(8,128)S(1)} async-done(((f32[16,32,1024]{2,1,0:T(8,128)}), f32[16,32,1024]{2,1,0:T(8,128)S(1)}, u32[]{:S(2)}, u32[]{:S(2)}) %all-to-all-start) | async-done | bytes 2097184 | tf_op jit(solution)/shard_map/all_to_all | solution.py:213
  60.6 15.9 %all_to_all.40 = f32[4,8,1024]{2,1,0:T(8,128)S(1)} all-to-all(f32[4,8,1024]{2,1,0:T(8,128)S(1)} %bitcast.43), channel_id=1, replica_groups=mesh['yl'=2,'core'=2,'x'=4,'zh'=4,'zl'=2,'yh'=2] {'zh'}, dimensions={0} | all-to-all | bytes 262144 | tf_op jit(solution)/shard_map/all_to_all | solution.py:215
  77.3 3.3 %all-to-all-start.2 = ((f32[4,8,1024]{2,1,0:T(8,128)}), f32[4,8,1024]{2,1,0:T(8,128)S(1)}, u32[]{:S(2)}, u32[]{:S(2)}) async-start(f32[4,8,1024]{2,1,0:T(8,128)} %broadcast_in_dim.23), calls=%async_computation.2 | async-start | bytes 262144 | tf_op jit(solution)/shard_map/all_to_all | solution.py:223
  80.6 7.2 %all-to-all-done.2 = f32[4,8,1024]{2,1,0:T(8,128)S(1)} async-done(((f32[4,8,1024]{2,1,0:T(8,128)}), f32[4,8,1024]{2,1,0:T(8,128)S(1)}, u32[]{:S(2)}, u32[]{:S(2)}) %all-to-all-start.2) | async-done | bytes 131104 | tf_op jit(solution)/shard_map/all_to_all | solution.py:223
  87.8 1.6 broadcast_in_dim.24
  89.4 4.4 %all-to-all-start.3 = ((f32[16,32,1024]{2,1,0:T(8,128)}), f32[16,32,1024]{2,1,0:T(8,128)S(1)}, u32[]{:S(2)}, u32[]{:S(2)}) async-start(f32[16,32,1024]{2,1,0:T(8,128)} %broadcast_in_dim.24), calls=%async_computation.4 | async-start | bytes 4194304 | tf_op jit(solution)/shard_map/all_to_all | solution.py:225
  94.5 31.6 %reduce-scatter.7.cloned.1.call-done = f32[32,512]{1,0:T(8,128)} async-done(((f32[128,512]{1,0:T(8,128)}), f32[32,512]{1,0:T(8,128)}) %reduce-scatter.7.cloned.1.call-update) | async-done | bytes 65552 | tf_op jit(solution)/shard_map/reduce_scatter | solution.py:230
  127.5 16.7 %attend.1 = (bf16[512,1024]{1,0:T(8,128)(2,1)}, bf16[512,1024]{1,0:T(8,128)(2,1)}, f32[512,1024]{1,0:T(8,128)}, f32[8,4,2,32,256]{4,3,2,1,0:T(8,128)}, f32[8,4,2,32,256]{4,3,2,1,0:T(8,128)}) custom-call(s32[1]{0:T(128)} %bitcast.core_ref, bf16[512,1024]{1,0:T(8,128)(2,1)} %get-tuple-element.24.q_ref, bf16[512,1024]{1,0:T(8,128)(2,1)} %bitcast.50, ...), custom_call_target="tpu_custom_call" | custom-call | flops 6442450944 | bytes 12582912 | tf_op jit(solution)/shard_map/attend/pallas_call | solution.py:138
  144.2 1.4 collective-permute-start.1
  145.7 2.5 collective-permute-start
  148.2 1.7 collective-permute-done
  150.0 7.9 %all-to-all-start.4 = ((f32[16,32,1024]{2,1,0:T(8,128)}), f32[16,32,1024]{2,1,0:T(8,128)S(1)}, u32[]{:S(2)}, u32[]{:S(2)}) async-start(f32[16,32,1024]{2,1,0:T(8,128)} %bitcast.36), calls=%async_computation.6 | async-start | bytes 4194304 | tf_op jit(solution)/shard_map/all_to_all | solution.py:213
  157.9 4.1 %add.43 = f32[8,4,2,32,256]{4,3,2,1,0:T(8,128)} add(f32[8,4,2,32,256]{4,3,2,1,0:T(8,128)} %get-tuple-element.35, f32[8,4,2,32,256]{4,3,2,1,0:T(8,128)} %collective-permute-done.1) | non-fusion elementwise | flops 524288 | bytes 6291456 | tf_op jit(solution)/shard_map/add | solution.py:266
  162.0 28.1 %all-to-all-done.4 = f32[16,32,1024]{2,1,0:T(8,128)S(1)} async-done(((f32[16,32,1024]{2,1,0:T(8,128)}), f32[16,32,1024]{2,1,0:T(8,128)S(1)}, u32[]{:S(2)}, u32[]{:S(2)}) %all-to-all-start.4) | async-done | bytes 2097184 | tf_op jit(solution)/shard_map/all_to_all | solution.py:213
  190.3 11.3 %all_to_all.41 = f32[4,8,1024]{2,1,0:T(8,128)S(1)} all-to-all(f32[4,8,1024]{2,1,0:T(8,128)S(1)} %bitcast.44), channel_id=1, replica_groups=mesh['yl'=2,'core'=2,'x'=4,'zh'=4,'zl'=2,'yh'=2] {'zh'}, dimensions={0} | all-to-all | bytes 262144 | tf_op jit(solution)/shard_map/all_to_all | solution.py:215
  201.7 10.1 %all_to_all.42 = f32[4,8,1024]{2,1,0:T(8,128)S(1)} all-to-all(f32[4,8,1024]{2,1,0:T(8,128)S(1)} %broadcast_in_dim.26), channel_id=1, replica_groups=mesh['yl'=2,'core'=2,'x'=4,'zh'=4,'zl'=2,'yh'=2] {'zh'}, dimensions={0} | all-to-all | bytes 262144 | tf_op jit(solution)/shard_map/all_to_all | solution.py:223
  211.7 1.6 broadcast_in_dim.27
  213.3 4.7 %all-to-all-start.7 = ((f32[16,32,1024]{2,1,0:T(8,128)}), f32[16,32,1024]{2,1,0:T(8,128)S(1)}, u32[]{:S(2)}, u32[]{:S(2)}) async-start(f32[16,32,1024]{2,1,0:T(8,128)} %broadcast_in_dim.27), calls=%async_computation.10 | async-start | bytes 4194304 | tf_op jit(solution)/shard_map/all_to_all | solution.py:225
  218.6 32.5 %reduce-scatter.11.cloned.1.call-done = f32[64,256]{1,0:T(8,128)} async-done(((f32[256,256]{1,0:T(8,128)}), f32[64,256]{1,0:T(8,128)}) %reduce-scatter.11.cloned.1.call-update) | async-done | bytes 65552 | tf_op jit(solution)/shard_map/reduce_scatter | solution.py:230
  252.4 2.9 %collective-permute-start.2 = (f32[2,16,256]{2,1,0:T(8,128)S(1)}, f32[2,16,256]{2,1,0:T(8,128)S(1)}, u32[]{:S(2)}, u32[]{:S(2)}) collective-permute-start(f32[2,16,256]{2,1,0:T(8,128)S(1)} %dynamic-slice_bitcast_fusion), channel_id=1, source_target_pairs={{0,1},{1,0},{2,3},{3,2},{4,5},{5,4},{6,7},{7,6},{8,9},{9,8},{10,11... | collective-permute-start | bytes 98312 | tf_op jit(solution)/shard_map/ppermute | solution.py:239
  256.8 2.6 collective-permute-start.3
  261.4 8.7 %input_grads.1 = bf16[512,1024]{1,0:T(8,128)(2,1)} custom-call(f32[512,1024]{1,0:T(8,128)} %bitcast.35, bf16[512,1024]{1,0:T(8,128)(2,1)} %get-tuple-element.40.dq_ref, bf16[256,512]{1,0:T(8,128)(2,1)} %kproj_ref.3, bf16[256,512]{1,0:T(8,128)(2,1)} %vproj_ref.3, bf16[1024,1024]{1,0:T(8,128)(2,1)} %wq_ref.3, bf16[1024,1024]{1,0:T(8,128)(2,1)} %wk_ref.3, ...), custom_call_target="tpu_custom_call" | custom-call | flops 3758096384 | bytes 11534336 | tf_op jit(solution)/shard_map/input_grads/pallas_call | solution.py:194
  (47 shorter events, 9.8 us)
Async XLA Ops:
  18.5 42.0 %all-to-all-start = ((f32[16,32,1024]{2,1,0:T(8,128)}), f32[16,32,1024]{2,1,0:T(8,128)S(1)}, u32[]{:S(2)}, u32[]{:S(2)}) async-start(f32[16,32,1024]{2,1,0:T(8,128)} %bitcast.40), calls=%async_computation | async-start | bytes 4194304 | tf_op jit(solution)/shard_map/all_to_all | solution.py:213
  27.5 53.1 %reduce-scatter.5.cloned.1.call-start = ((), (), s32[]{:S(2)}) async-start(), calls=%async_computation.12 | async-start | bytes 2359296 | tf_op jit(solution)/shard_map/reduce_scatter | solution.py:230
  77.3 10.6 %all-to-all-start.2 = ((f32[4,8,1024]{2,1,0:T(8,128)}), f32[4,8,1024]{2,1,0:T(8,128)S(1)}, u32[]{:S(2)}, u32[]{:S(2)}) async-start(f32[4,8,1024]{2,1,0:T(8,128)} %broadcast_in_dim.23), calls=%async_computation.2 | async-start | bytes 262144 | tf_op jit(solution)/shard_map/all_to_all | solution.py:223
  89.4 36.7 %all-to-all-start.3 = ((f32[16,32,1024]{2,1,0:T(8,128)}), f32[16,32,1024]{2,1,0:T(8,128)S(1)}, u32[]{:S(2)}, u32[]{:S(2)}) async-start(f32[16,32,1024]{2,1,0:T(8,128)} %broadcast_in_dim.24), calls=%async_computation.4 | async-start | bytes 4194304 | tf_op jit(solution)/shard_map/all_to_all | solution.py:225
  93.8 32.4 %reduce-scatter.7.cloned.1.call-start = ((), (), s32[]{:S(2)}) async-start(), calls=%async_computation.13 | async-start | bytes 327680 | tf_op jit(solution)/shard_map/reduce_scatter | solution.py:230
  126.2 1.3 copy-start.1
  127.5 18.2 %copy-start.2 = (f32[32,512]{1,0:T(8,128)S(1)}, f32[32,512]{1,0:T(8,128)}, u32[]{:S(2)}) copy-start(f32[32,512]{1,0:T(8,128)} %reduce-scatter.7.cloned.1.call-done) | copy-start | bytes 196612
  144.2 13.7 %collective-permute-start.1 = (f32[8,4,2,32,256]{4,3,2,1,0:T(8,128)}, f32[8,4,2,32,256]{4,3,2,1,0:T(8,128)}, u32[]{:S(2)}, u32[]{:S(2)}) collective-permute-start(f32[8,4,2,32,256]{4,3,2,1,0:T(8,128)} %get-tuple-element.36), channel_id=1, source_target_pairs={{0,64},{64,0},{1,65},{65,1},{2,66},{66,2},{3,67},{67,3},{4,68},{68... | collective-permute-start | bytes 6291464 | tf_op jit(solution)/shard_map/ppermute | solution.py:266
  145.7 4.3 %collective-permute-start = (f32[16,512]{1,0:T(8,128)S(1)}, f32[16,512]{1,0:T(8,128)S(1)}, u32[]{:S(2)}, u32[]{:S(2)}) collective-permute-start(f32[16,512]{1,0:T(8,128)S(1)} %dynamic-slice_bitcast_fusion.1), channel_id=1, source_target_pairs={{0,1},{1,0},{2,3},{3,2},{4,5},{5,4},{6,7},{7,6},{8,9},{9,8},{10,11... | collective-permute-start | bytes 98312 | tf_op jit(solution)/shard_map/ppermute | solution.py:239
  150.0 40.2 %all-to-all-start.4 = ((f32[16,32,1024]{2,1,0:T(8,128)}), f32[16,32,1024]{2,1,0:T(8,128)S(1)}, u32[]{:S(2)}, u32[]{:S(2)}) async-start(f32[16,32,1024]{2,1,0:T(8,128)} %bitcast.36), calls=%async_computation.6 | async-start | bytes 4194304 | tf_op jit(solution)/shard_map/all_to_all | solution.py:213
  157.8 53.9 %reduce-scatter.9.cloned.1.call-start = ((), (), s32[]{:S(2)}) async-start(), calls=%async_computation.14 | async-start | bytes 2359296 | tf_op jit(solution)/shard_map/reduce_scatter | solution.py:230
  213.3 37.8 %all-to-all-start.7 = ((f32[16,32,1024]{2,1,0:T(8,128)}), f32[16,32,1024]{2,1,0:T(8,128)S(1)}, u32[]{:S(2)}, u32[]{:S(2)}) async-start(f32[16,32,1024]{2,1,0:T(8,128)} %broadcast_in_dim.27), calls=%async_computation.10 | async-start | bytes 4194304 | tf_op jit(solution)/shard_map/all_to_all | solution.py:225
  218.0 33.1 %reduce-scatter.11.cloned.1.call-start = ((), (), s32[]{:S(2)}) async-start(), calls=%async_computation.15 | async-start | bytes 327680 | tf_op jit(solution)/shard_map/reduce_scatter | solution.py:230
  251.1 1.3 copy-start
  251.1 1.3 copy-start.3
  252.4 4.3 %collective-permute-start.2 = (f32[2,16,256]{2,1,0:T(8,128)S(1)}, f32[2,16,256]{2,1,0:T(8,128)S(1)}, u32[]{:S(2)}, u32[]{:S(2)}) collective-permute-start(f32[2,16,256]{2,1,0:T(8,128)S(1)} %dynamic-slice_bitcast_fusion), channel_id=1, source_target_pairs={{0,1},{1,0},{2,3},{3,2},{4,5},{5,4},{6,7},{7,6},{8,9},{9,8},{10,11... | collective-permute-start | bytes 98312 | tf_op jit(solution)/shard_map/ppermute | solution.py:239
  256.8 3.7 %collective-permute-start.3 = (f32[48,1024]{1,0:T(8,128)S(1)}, f32[48,1024]{1,0:T(8,128)S(1)}, u32[]{:S(2)}, u32[]{:S(2)}) collective-permute-start(f32[48,1024]{1,0:T(8,128)S(1)} %maximum_multiply_fusion), channel_id=1, source_target_pairs={{0,64},{64,0},{1,65},{65,1},{2,66},{66,2},{3,67},{67,3},{4,68},{68... | collective-permute-start | bytes 589832 | tf_op jit(solution)/shard_map/ppermute | solution.py:243
  260.5 9.6 %collective-permute-start.4 = (f32[48,1024]{1,0:T(8,128)S(1)}, f32[48,1024]{1,0:T(8,128)S(1)}, u32[]{:S(2)}, u32[]{:S(2)}) collective-permute-start(f32[48,1024]{1,0:T(8,128)S(1)} %fusion.12), channel_id=1, source_target_pairs={{0,128},{128,0},{1,129},{129,1},{2,130},{130,2},{3,131},{131,3},{4... | collective-permute-start | bytes 589832 | tf_op jit(solution)/shard_map/ppermute | solution.py:243
Sparse Core Ops, SparseCore 0:
  30.8 47.6 reduce-scatter.4
  97.1 28.9 reduce-scatter.6
  162.1 44.4 reduce-scatter.8
  221.2 29.8 reduce-scatter.10

commit v4 on v3

v4 whole, which is shorter than its diff:
```python
import functools
import math

import jax
import jax.numpy as jnp
from jax import lax
from jax.experimental import pallas as pl
from jax.experimental.pallas import tpu as pltpu
from jax.sharding import Mesh
from jax.sharding import PartitionSpec as P

HEADS = 16
HEAD_DIM = 64
SPLITS = {64: (4, 4, 2, 2), 8: (4, 2, 1, 1)}
SEQ = ("x", "zh", "zl", "yh")
Z = ("zh", "zl")
NEAR = ("x", "yh")
VMEM_LIMIT = 60 * 1024 * 1024
LAST_VMEM = 18 * 1024 * 1024


def dot(a, b):
    return jnp.dot(a, b, preferred_element_type=jnp.float32)


def dot_t(a, b):
    return lax.dot_general(a, b, (((1,), (1,)), ((), ())), preferred_element_type=jnp.float32)


def project_kernel(
    x_ref, wq_ref, wk_ref, wv_ref, kproj_ref, vproj_ref, query_ref, part_ref, xt_ref, seen_ref, projt_ref
):
    width = query_ref.shape[1]
    proj = kproj_ref.shape[0]

    @pl.when(pl.program_id(0) == 0)
    def _():
        projt_ref[:, :proj] = kproj_ref[...].T
        projt_ref[:, proj:] = vproj_ref[...].T

    x = x_ref[...]
    columns = pl.ds(pl.multiple_of(pl.program_id(0) * width, width), width)
    xt = x_ref[:, columns].T
    xt_ref[...] = xt
    n_z, _, chunk, _ = seen_ref.shape
    seen_ref[:, 0] = dot(xt, projt_ref[...]).reshape(n_z, chunk, 2 * proj)
    weights = jnp.concatenate([wk_ref[...], wv_ref[...], wq_ref[...]], axis=1)
    out = dot(x, weights).astype(jnp.bfloat16)
    part_ref[:proj] = dot(kproj_ref[...], out[:, :width])
    part_ref[proj:] = dot(vproj_ref[...], out[:, width : 2 * width])
    query_ref[...] = out[:, 2 * width :]


def project(inputs, w_query, w_key, w_value, key_proj, value_proj):
    rows, width = inputs.shape
    proj = key_proj.shape[0]
    n_x, n_z = lax.axis_size("x"), lax.axis_size(Z)
    block = width // n_x
    whole = lambda a: pl.BlockSpec(a.shape, lambda i: (0, 0))
    weight = pl.BlockSpec((width, block), lambda i: (0, i))
    return pl.pallas_call(
        project_kernel,
        grid=(n_x,),
        in_specs=[whole(inputs), weight, weight, weight, whole(key_proj), whole(value_proj)],
        out_specs=[
            pl.BlockSpec((rows, block), lambda i: (0, i)),
            pl.BlockSpec((2 * proj, block), lambda i: (0, i)),
            pl.BlockSpec((block, rows), lambda i: (i, 0)),
            pl.BlockSpec((n_z, 1, block // n_z, 2 * proj), lambda i: (0, i, 0, 0)),
        ],
        out_shape=[
            jax.ShapeDtypeStruct((rows, width), jnp.bfloat16),
            jax.ShapeDtypeStruct((2 * proj, width), jnp.float32),
            jax.ShapeDtypeStruct((width, rows), jnp.bfloat16),
            jax.ShapeDtypeStruct((n_z, n_x, block // n_z, 2 * proj), jnp.float32),
        ],
        scratch_shapes=[pltpu.VMEM((rows, 2 * proj), jnp.bfloat16)],
        compiler_params=pltpu.CompilerParams(vmem_limit_bytes=VMEM_LIMIT),
        cost_estimate=pl.CostEstimate(
            flops=2 * rows * width * (3 * width + 4 * proj), bytes_accessed=14 << 20, transcendentals=0
        ),
        name="project",
    )(inputs, w_query, w_key, w_value, key_proj, value_proj)


def attend_kernel(
    norm, core_ref, q_ref, c_ref, ks_ref, vs_ref, xt_ref, att_ref, dq_ref, dsum_ref, other_ref, mine_ref
):
    step = pl.program_id(0)
    block = q_ref.shape[1]
    proj = ks_ref.shape[0] * ks_ref.shape[1]
    rows = q_ref.shape[0]
    scale = 1.0 / math.sqrt(HEAD_DIM)
    q, c = q_ref[...], c_ref[...]
    qt, ct = q.T, c.T
    kp32 = (ks_ref[...].reshape(proj, block) * norm).astype(jnp.bfloat16).astype(jnp.float32)
    vp32 = (vs_ref[...].reshape(proj, block) * norm).astype(jnp.bfloat16).astype(jnp.float32)
    kpt = kp32.T.astype(jnp.bfloat16)
    vpt = vp32.T.astype(jnp.bfloat16)
    kps = kp32 * scale
    lane = lax.broadcasted_iota(jnp.int32, (proj, block), 1)
    att, dq = [], []
    dk = dv = None
    for h in range(block // HEAD_DIM):
        mine = (lane >= h * HEAD_DIM) & (lane < (h + 1) * HEAD_DIM)
        sub = slice(h * HEAD_DIM, (h + 1) * HEAD_DIM)
        scores = dot(jnp.where(mine, kps, 0.0).astype(jnp.bfloat16), qt)
        dprob = dot(jnp.where(mine, vp32, 0.0).astype(jnp.bfloat16), ct)
        low, dscore = [], []
        for at in range(0, rows, 128):
            s, d = scores[:, at : at + 128], dprob[:, at : at + 128]
            e = jnp.exp(s - jnp.max(s, axis=0, keepdims=True))
            p = e * (1.0 / jnp.sum(e, axis=0, keepdims=True))
            low.append(p.astype(jnp.bfloat16))
            dscore.append((p * (d - jnp.sum(p * d, axis=0, keepdims=True))).astype(jnp.bfloat16))
        low, dscore = jnp.concatenate(low, axis=1), jnp.concatenate(dscore, axis=1)
        att.append(dot(vpt[sub], low))
        dq.append(dot(kpt[sub], dscore))
        dk_h, dv_h = dot(dscore, q), dot(low, c)
        dk, dv = (dk_h, dv_h) if h == 0 else (jnp.where(mine, dk_h, dk), jnp.where(mine, dv_h, dv))
    att_ref[...] = jnp.concatenate(att, axis=0).T.astype(jnp.bfloat16)
    dquery = (jnp.concatenate(dq, axis=0) * scale).T.astype(jnp.bfloat16)
    dq_ref[...] = dquery
    dsum_ref[:proj] = dk * scale
    dsum_ref[proj:] = dv

    def put(ref):
        n_z, n_x, _, chunk, _ = ref.shape
        for x in range(n_x):
            rows = n_z * chunk
            term = dot(xt_ref[x * rows : (x + 1) * rows], dquery)
            ref[:, x, 0] = term.reshape(n_z, chunk, block)

    pl.when(step < 2)(functools.partial(put, other_ref))
    pl.when(step >= 2)(functools.partial(put, mine_ref))


def attend(query, cotangent, sums, inputs_t, norm, both):
    rows, width = query.shape
    proj = both // 2
    plane = sums.shape[0]
    n_x, n_z = lax.axis_size("x"), lax.axis_size(Z)
    block = width // 4
    core = lax.axis_index("core").astype(jnp.int32).reshape(1)
    place = lambda i, core: lax.rem(i + 2 * (1 - core[0]), 4)
    tokens = pl.BlockSpec((rows, block), lambda i, core: (0, place(i, core)))
    terms = (n_z, n_x, 2, width // (n_x * n_z), block)
    terms_block = (n_z, n_x, 1, width // (n_x * n_z), block)
    return pl.pallas_call(
        functools.partial(attend_kernel, norm),
        grid_spec=pltpu.PrefetchScalarGridSpec(
            num_scalar_prefetch=1,
            grid=(4,),
            in_specs=[
                tokens,
                tokens,
                pl.BlockSpec((plane // 2, both // plane, block), lambda i, core: (0, 0, place(i, core))),
                pl.BlockSpec((plane // 2, both // plane, block), lambda i, core: (1, 0, place(i, core))),
                pl.BlockSpec((width, rows), lambda i, core: (0, 0)),
            ],
            out_specs=[
                tokens,
                tokens,
                pl.BlockSpec((2 * proj, block), lambda i, core: (0, place(i, core))),
                pl.BlockSpec(terms_block, lambda i, core: (0, 0, jnp.minimum(i, 1), 0, 0)),
                pl.BlockSpec(terms_block, lambda i, core: (0, 0, jnp.maximum(i - 2, 0), 0, 0)),
            ],
        ),
        out_shape=[
            jax.ShapeDtypeStruct((rows, width), jnp.bfloat16),
            jax.ShapeDtypeStruct((rows, width), jnp.bfloat16),
            jax.ShapeDtypeStruct((2 * proj, width), jnp.float32),
            jax.ShapeDtypeStruct(terms, jnp.float32),
            jax.ShapeDtypeStruct(terms, jnp.float32),
        ],
        compiler_params=pltpu.CompilerParams(vmem_limit_bytes=VMEM_LIMIT),
        cost_estimate=pl.CostEstimate(
            flops=8 * rows * width * proj * 6, bytes_accessed=12 << 20, transcendentals=rows * HEADS * proj
        ),
        name="attend",
    )(core, query, cotangent, sums, sums, inputs_t)


def input_grads_kernel(
    norm, sums_ref, dq_ref, kproj_ref, vproj_ref, wq_ref, wk_ref, wv_ref, out_ref, dkeys_ref, dvalues_ref
):
    proj = kproj_ref.shape[0]

    @pl.when(pl.program_id(0) == 0)
    def _():
        both = sums_ref[...].reshape(2 * proj, -1) * norm
        dkp = both[:proj].astype(jnp.bfloat16)
        dkeys_ref[...] = dot(kproj_ref[...].T, dkp).astype(jnp.bfloat16)
        dvp = both[proj:].astype(jnp.bfloat16)
        dvalues_ref[...] = dot(vproj_ref[...].T, dvp).astype(jnp.bfloat16)

    grad = dot_t(dq_ref[...], wq_ref[...]) + dot_t(dkeys_ref[...], wk_ref[...])
    out_ref[...] = (grad + dot_t(dvalues_ref[...], wv_ref[...])).astype(jnp.bfloat16)


def input_grads(sums, dquery, key_proj, value_proj, w_query, w_key, w_value, norm):
    rows, width = dquery.shape
    block = width // 4
    plane, both = sums.shape[0], 2 * key_proj.shape[0]
    whole = lambda a: pl.BlockSpec(a.shape, lambda i: (0, 0))
    weight = pl.BlockSpec((block, width), lambda i: (i, 0))
    return pl.pallas_call(
        functools.partial(input_grads_kernel, norm),
        grid=(4,),
        in_specs=[
            pl.BlockSpec((plane, both // plane, width), lambda i: (0, 0, 0)),
            whole(dquery),
            whole(key_proj),
            whole(value_proj),
            weight,
            weight,
            weight,
        ],
        out_specs=pl.BlockSpec((rows, block), lambda i: (0, i)),
        out_shape=jax.ShapeDtypeStruct((rows, width), jnp.bfloat16),
        scratch_shapes=[pltpu.VMEM((rows, width), jnp.bfloat16)] * 2,
        compiler_params=pltpu.CompilerParams(vmem_limit_bytes=LAST_VMEM),
        cost_estimate=pl.CostEstimate(
            flops=2 * rows * width * (3 * width + both), bytes_accessed=11 << 20, transcendentals=0
        ),
        name="input_grads",
    )(sums, dquery, key_proj, value_proj, w_query, w_key, w_value)


def scatter_sum(part):
    rows, width = part.shape
    plane = lax.axis_size(NEAR)
    depth = lax.axis_size(Z)
    got = lax.all_to_all(part.reshape(plane, rows // plane, width), NEAR, 0, 0)
    mine = jnp.sum(got, axis=0)
    got = lax.all_to_all(mine.reshape(depth, rows // plane // depth, width), Z, 0, 0)
    return jnp.sum(got, axis=0)


def gather_rows(mine, extra):
    rows, width = mine.shape
    plane = lax.axis_size(NEAR)
    depth = lax.axis_size(Z)
    got = lax.all_to_all(jnp.broadcast_to(mine, (depth, rows, width)), Z, 0, 0)
    got, extra = lax.optimization_barrier((got.reshape(depth * rows, width), extra))
    got = jnp.broadcast_to(got, (plane, depth * rows, width))
    got = lax.all_to_all(jnp.concatenate([got, extra], axis=1), NEAR, 0, 0)
    return got, jnp.sum(got[:, depth * rows :], axis=0)


def scatter_rows(part, axis):
    return lax.psum_scatter(part, axis, scatter_dimension=0, tiled=True)


def body(inputs, w_query, w_key, w_value, key_proj, value_proj, cotangent):
    inputs, cotangent = inputs[0], cotangent[0]
    rows, width = inputs.shape
    proj = key_proj.shape[0]
    n_seq = lax.axis_size(SEQ)
    n_x, n_yh = lax.axis_size("x"), lax.axis_size("yh")
    n_data = lax.axis_size(("yl", "core"))
    norm = 1.0 / math.sqrt(rows * n_seq)
    factor = 1.0 / math.sqrt(rows * n_seq * n_data)

    query, part, inputs_t, seen = project(inputs, w_query, w_key, w_value, key_proj, value_proj)
    seen = scatter_rows(seen.reshape(width, 2 * proj), Z)
    half = width // n_seq // 2
    seen = jnp.swapaxes(seen.reshape(n_x * n_yh, 2, half, 2 * proj), 1, 2)
    sums, seen = gather_rows(scatter_sum(part), seen.reshape(n_x * n_yh, half, -1))
    seen = jnp.swapaxes(seen.reshape(half, 2, 2 * proj), 0, 1).reshape(-1, 2 * proj)

    attended, dquery, part, other, mine = attend(query, cotangent, sums, inputs_t, norm, 2 * proj)

    grad_q = mine + lax.ppermute(other, "core", [(0, 1), (1, 0)])
    grad_q = scatter_rows(grad_q.reshape(-1, width // n_data), Z)
    grad_q = grad_q.reshape(n_x, 2, n_yh, 2, half, width // n_data).transpose(0, 2, 4, 1, 3, 5)
    sums, grad_q = gather_rows(scatter_sum(part), grad_q.reshape(n_x * n_yh, half, -1))
    grad_q = grad_q.reshape(half, 2, 2, width // n_data).transpose(2, 0, 1, 3).reshape(2 * half, -1)

    low = sums[:, : 2 * proj // (n_x * n_yh)].reshape(2 * proj, width)
    low = (low * norm).astype(jnp.bfloat16)
    dkp_low, dvp_low = low[:proj], low[proj:]
    seen_high = seen.astype(jnp.bfloat16)
    seen_low = (seen - seen_high.astype(jnp.float32)).astype(jnp.bfloat16)
    grad_k = dot(seen_high[:, :proj], dkp_low) + dot(seen_low[:, :proj], dkp_low)
    grad_v = dot(seen_high[:, proj:], dvp_low) + dot(seen_low[:, proj:], dvp_low)
    core = lax.axis_index("core")
    grad_q = jnp.concatenate([jnp.where(core == i, grad_q, 0.0) for i in range(2)], axis=1)
    grads = jnp.concatenate([grad_q, grad_k, grad_v], axis=0) * factor
    across = [lax.ppermute(grads, ("yl", "core"), [(i, i ^ d) for i in range(4)]) for d in (1, 2, 3)]
    grad_inputs = input_grads(sums, dquery, key_proj, value_proj, w_query, w_key, w_value, norm)
    grads = (grads + across[0]) + (across[1] + across[2])
    grad_q, grad_k, grad_v = jnp.split(grads, 3, axis=0)

    return (attended[None], grad_inputs[None], grad_q, grad_k, grad_v)


def solution(mesh):
    split = SPLITS[mesh.shape["seq"]]
    fine = Mesh(mesh.devices.reshape((2, 2) + split), ("yl", "core") + SEQ)
    tokens = P(("yl", "core"), SEQ, None)
    return jax.shard_map(
        body,
        mesh=fine,
        in_specs=(tokens, P(), P(), P(), P(None, SEQ), P(None, SEQ), tokens),
        out_specs=(tokens, tokens, P(SEQ, None), P(SEQ, None), P(SEQ, None)),
        check_vma=False,
    )
```

time: 278 us -> 271 us (0.975)
  blocking collectives: 37.3 us -> 108 us
  waiting for transfers between devices: 137 us -> 74.9 us
  starting transfers between devices: 39.8 us -> 20.9 us
  Pallas kernels: 36.8 us -> 31.9 us
  local copies, waits for them, and re-layouts: 6.57 us -> 11.1 us
  other arithmetic: 4.73 us -> 8.17 us
    all_to_all x3 -> x5, blocking collectives: 37.3 us -> 108 us  [the longest x2 65.3 us: scatter_sum(): got = lax.all_to_all(part.reshape(plane, rows // plane, width), NEAR, 0, 0)]
    reduce_scatter x4 -> x2, waiting for transfers between devices: 64.1 us -> 0.02 us  [scatter_rows(): return lax.psum_scatter(part, axis, scatter_dimension=0, tiled=True)]
    all_to_all x5 -> x3, starting transfers between devices: 29.2 us -> 13.7 us  [the longest x2 10.3 us: gather_rows(): got = lax.all_to_all(jnp.concatenate([got, extra], axis=1), NEAR, 0, 0)]
    unnamed x8 -> x16, local copies, waits for them, and re-layouts: 2.04 us -> 8.11 us
    ppermute x4 -> x3, starting transfers between devices: 8.96 us -> 4.42 us  [body(): lax.ppermute(grads, ('yl', 'core'), [(i, i ^ d) for i in range(4)])]
    ppermute x1, waiting for transfers between devices: 0.01 us -> 4 us  [body(): grad_q = mine + lax.ppermute(other, 'core', [(0, 1), (1, 0)])]
    ppermute x4 -> x3, waiting for transfers between devices: 3.79 us -> 0.01 us  [body(): lax.ppermute(grads, ('yl', 'core'), [(i, i ^ d) for i in range(4)])]
    all_to_all x5 -> x3, waiting for transfers between devices: 67.7 us -> 70.9 us  [the longest x2 62.5 us: gather_rows(): got = lax.all_to_all(jnp.concatenate([got, extra], axis=1), NEAR, 0, 0)]
  transfers between devices with their start and end apart: 14 -> 9, of which waited for: 8 -> 4; matrix products, arithmetic and copies ran while one was open for 2% -> 1% of each run, Pallas kernels for 3% -> 2%
where the time goes in v4:
time: 271 us; the launch traced here: 270 us
  blocking collectives  108 us (40%)
  waiting for transfers between devices  74.9 us (28%)
  Pallas kernels  31.9 us (12%)
  starting transfers between devices  20.9 us (8%)
  between operations  14.2 us (5%)
  local copies, waits for them, and re-layouts  11.1 us (4%)
  other arithmetic  8.17 us (3%)
    all_to_all x2, blocking collectives, scatter_sum(): got = lax.all_to_all(part.reshape(plane, rows // plane, width), NEAR, 0, 0)  65.3 us
    all_to_all x2, waiting for transfers between devices, gather_rows(): got = lax.all_to_all(jnp.concatenate([got, extra], axis=1), NEAR, 0, 0)  62.5 us
    all_to_all x2, blocking collectives, scatter_sum(): lax.all_to_all(mine.reshape(depth, rows // plane // depth, width), Z, 0, 0)  31 us
    pallas_call x1, Pallas kernels, attend(): pl.pallas_call(functools.partial(attend_kernel, norm), grid_spec=pltpu.Pr...  16.8 us
    all_to_all x1, blocking collectives, gather_rows(): got = lax.all_to_all(jnp.broadcast_to(mine, (depth, rows, width)), Z, 0, 0)  11.9 us
    all_to_all x2, starting transfers between devices, gather_rows(): got = lax.all_to_all(jnp.concatenate([got, extra], axis=1), NEAR, 0, 0)  10.3 us
    pallas_call x1, Pallas kernels, project(): pl.pallas_call(project_kernel, grid=(n_x,), in_specs=[whole(inputs), weig...  9.39 us
    all_to_all x1, waiting for transfers between devices, gather_rows(): got = lax.all_to_all(jnp.broadcast_to(mine, (depth, rows, width)), Z, 0, 0)  8.35 us
  transfers between devices with their start and end apart: 9, of which 4 were waited for; matrix products, arithmetic and copies ran while one was open for 1% of the time, Pallas kernels for 2%

profile of v4, /device:TPU:1, one launch (start us, length us, event | category | flops | bytes accessed | tf_op | source)
XLA Modules:
  0.0 270.1 jit_solution(7263334833956498279)
XLA Ops:
  7.2 9.4 %project.1 = (bf16[512,1024]{1,0:T(8,128)(2,1)}, f32[512,1024]{1,0:T(8,128)}, bf16[1024,512]{1,0:T(8,128)(2,1)}, f32[8,4,32,512]{3,2,1,0:T(8,128)}) custom-call(bf16[512,1024]{1,0:T(8,128)(2,1)} %bitcast.59, bf16[1024,1024]{1,0:T(8,128)(2,1)} %wq_ref.3, bf16[1024,1024]{1,0:T(8,128)(2,1)} %wk_ref.3, bf16[1024,1024]{1,0:T(8,128)(2,1)} %wv_ref.3, ...), custom_call_target="tpu_custom_call" | custom-call | flops 4294967296 | bytes 14680064 | tf_op jit(solution)/shard_map/project/pallas_call | solution.py:61
  16.6 34.0 %all_to_all.40 = f32[8,64,1024]{2,1,0:T(8,128)S(1)} all-to-all(f32[8,64,1024]{2,1,0:T(8,128)} %bitcast.44), channel_id=1, replica_groups=mesh['yl'=2,'core'=2,'x'=4,'zh'=4,'zl'=2,'yh'=2] {'x','yh'}, dimensions={0} | all-to-all | bytes 4194304 | tf_op jit(solution)/shard_map/all_to_all | solution.py:234
  50.8 17.4 %all_to_all.41 = f32[8,8,1024]{2,1,0:T(8,128)S(1)} all-to-all(f32[8,8,1024]{2,1,0:T(8,128)S(1)} %bitcast.48), channel_id=1, replica_groups=mesh['yl'=2,'core'=2,'x'=4,'zh'=4,'zl'=2,'yh'=2] {'zh','zl'}, dimensions={0} | all-to-all | bytes 524288 | tf_op jit(solution)/shard_map/all_to_all | solution.py:236
  68.3 11.9 %all_to_all.42 = f32[8,8,1024]{2,1,0:T(8,128)S(1)} all-to-all(f32[8,8,1024]{2,1,0:T(8,128)S(1)} %broadcast_in_dim.23), channel_id=1, replica_groups=mesh['yl'=2,'core'=2,'x'=4,'zh'=4,'zl'=2,'yh'=2] {'zh','zl'}, dimensions={0} | all-to-all | bytes 524288 | tf_op jit(solution)/shard_map/all_to_all | solution.py:244
  81.1 1.6 pad_maximum_fusion
  82.7 5.8 %all-to-all-start.3 = ((f32[8,72,1024]{2,1,0:T(8,128)}), f32[8,72,1024]{2,1,0:T(8,128)S(1)}, u32[]{:S(2)}, u32[]{:S(2)}) async-start(f32[8,72,1024]{2,1,0:T(8,128)} %pad_maximum_fusion), calls=%async_computation.4 | async-start | bytes 4718592 | tf_op jit(solution)/shard_map/all_to_all | solution.py:247
  88.5 31.7 %all-to-all-done.3.ks_ref.vs_ref = f32[8,72,1024]{2,1,0:T(8,128)S(1)} async-done(((f32[8,72,1024]{2,1,0:T(8,128)}), f32[8,72,1024]{2,1,0:T(8,128)S(1)}, u32[]{:S(2)}, u32[]{:S(2)}) %all-to-all-start.3) | async-done | bytes 2359328 | tf_op jit(solution)/shard_map/all_to_all | solution.py:247
  120.2 1.4 copy-done.6
  121.6 16.8 %attend.1 = (bf16[512,1024]{1,0:T(8,128)(2,1)}, bf16[512,1024]{1,0:T(8,128)(2,1)}, f32[512,1024]{1,0:T(8,128)}, f32[8,4,2,32,256]{4,3,2,1,0:T(8,128)}, f32[8,4,2,32,256]{4,3,2,1,0:T(8,128)}) custom-call(s32[1]{0:T(128)} %bitcast.core_ref, bf16[512,1024]{1,0:T(8,128)(2,1)} %get-tuple-element.18.q_ref, bf16[512,1024]{1,0:T(8,128)(2,1)} %bitcast.60, ...), custom_call_target="tpu_custom_call" | custom-call | flops 6442450944 | bytes 12582912 | tf_op jit(solution)/shard_map/attend/pallas_call | solution.py:149
  138.5 2.7 collective-permute-start
  141.1 4.0 %collective-permute-done = f32[8,4,2,32,256]{4,3,2,1,0:T(8,128)S(1)} collective-permute-done((f32[8,4,2,32,256]{4,3,2,1,0:T(8,128)}, f32[8,4,2,32,256]{4,3,2,1,0:T(8,128)S(1)}, u32[]{:S(2)}, u32[]{:S(2)}) %collective-permute-start) | collective-permute-done | bytes 2097184 | tf_op jit(solution)/shard_map/ppermute | solution.py:274
  145.1 3.4 %add.22 = f32[8,4,2,32,256]{4,3,2,1,0:T(8,128)} add(f32[8,4,2,32,256]{4,3,2,1,0:T(8,128)} %get-tuple-element.26, f32[8,4,2,32,256]{4,3,2,1,0:T(8,128)S(1)} %collective-permute-done) | non-fusion elementwise | flops 524288 | bytes 6291456 | tf_op jit(solution)/shard_map/add | solution.py:274
  148.5 31.2 %all_to_all.43 = f32[8,64,1024]{2,1,0:T(8,128)S(1)} all-to-all(f32[8,64,1024]{2,1,0:T(8,128)} %bitcast.42), channel_id=1, replica_groups=mesh['yl'=2,'core'=2,'x'=4,'zh'=4,'zl'=2,'yh'=2] {'x','yh'}, dimensions={0} | all-to-all | bytes 4194304 | tf_op jit(solution)/shard_map/all_to_all | solution.py:234
  179.9 13.6 %all_to_all.44 = f32[8,8,1024]{2,1,0:T(8,128)S(1)} all-to-all(f32[8,8,1024]{2,1,0:T(8,128)S(1)} %bitcast.49), channel_id=1, replica_groups=mesh['yl'=2,'core'=2,'x'=4,'zh'=4,'zl'=2,'yh'=2] {'zh','zl'}, dimensions={0} | all-to-all | bytes 524288 | tf_op jit(solution)/shard_map/all_to_all | solution.py:236
  194.2 3.4 %all-to-all-start.6 = ((f32[8,8,1024]{2,1,0:T(8,128)}), f32[8,8,1024]{2,1,0:T(8,128)S(1)}, u32[]{:S(2)}, u32[]{:S(2)}) async-start(f32[8,8,1024]{2,1,0:T(8,128)} %broadcast_in_dim.26), calls=%async_computation.7 | async-start | bytes 524288 | tf_op jit(solution)/shard_map/all_to_all | solution.py:244
  198.6 8.4 %all-to-all-done.6 = f32[8,8,1024]{2,1,0:T(8,128)S(1)} async-done(((f32[8,8,1024]{2,1,0:T(8,128)}), f32[8,8,1024]{2,1,0:T(8,128)S(1)}, u32[]{:S(2)}, u32[]{:S(2)}) %all-to-all-start.6) | async-done | bytes 262176 | tf_op jit(solution)/shard_map/all_to_all | solution.py:244
  207.2 1.6 pad_maximum_fusion.1
  208.8 4.5 %all-to-all-start.7 = ((f32[8,72,1024]{2,1,0:T(8,128)}), f32[8,72,1024]{2,1,0:T(8,128)S(1)}, u32[]{:S(2)}, u32[]{:S(2)}) async-start(f32[8,72,1024]{2,1,0:T(8,128)} %pad_maximum_fusion.1), calls=%async_computation.9 | async-start | bytes 4718592 | tf_op jit(solution)/shard_map/all_to_all | solution.py:247
  214.3 30.8 %all-to-all-done.7.sums_ref = f32[8,72,1024]{2,1,0:T(8,128)S(1)} async-done(((f32[8,72,1024]{2,1,0:T(8,128)}), f32[8,72,1024]{2,1,0:T(8,128)S(1)}, u32[]{:S(2)}, u32[]{:S(2)}) %all-to-all-start.7) | async-done | bytes 2359328 | tf_op jit(solution)/shard_map/all_to_all | solution.py:247
  246.4 2.7 collective-permute-start.1
  250.8 1.6 copy-done
  252.4 1.6 copy-done.1
  254.0 1.6 copy-done.2
  256.8 5.7 %input_grads.1 = bf16[512,1024]{1,0:T(8,128)(2,1)} custom-call(f32[8,72,1024]{2,1,0:T(8,128)S(1)} %all-to-all-done.7.sums_ref, bf16[512,1024]{1,0:T(8,128)(2,1)S(1)} %copy-done.5, bf16[256,512]{1,0:T(8,128)(2,1)S(1)} %copy-done.3, bf16[256,512]{1,0:T(8,128)(2,1)S(1)} %copy-done.4, bf16[1024,1024]{1,0:T(8,128)(2,1)S(1)} %copy-done, ...), custom_call_target="tpu_custom_call" | custom-call | flops 3758096384 | bytes 11534336 | tf_op jit(solution)/shard_map/input_grads/pallas_call | solution.py:207
  (49 shorter events, 9.2 us)
Async XLA Ops:
  7.2 73.0 %reduce-scatter.3.cloned.1.call-start = ((), (), s32[]{:S(2)}) async-start(), calls=%async_computation.10 | async-start | bytes 2359296 | tf_op jit(solution)/shard_map/reduce_scatter | solution.py:252
  80.1 1.0 copy-start.7
  82.7 37.5 %all-to-all-start.3 = ((f32[8,72,1024]{2,1,0:T(8,128)}), f32[8,72,1024]{2,1,0:T(8,128)S(1)}, u32[]{:S(2)}, u32[]{:S(2)}) async-start(f32[8,72,1024]{2,1,0:T(8,128)} %pad_maximum_fusion), calls=%async_computation.4 | async-start | bytes 4718592 | tf_op jit(solution)/shard_map/all_to_all | solution.py:247
  88.5 109.2 %reduce-scatter.5.cloned.1.call-start = ((), (), s32[]{:S(2)}) async-start(), calls=%async_computation.11 | async-start | bytes 2359296 | tf_op jit(solution)/shard_map/reduce_scatter | solution.py:252
  120.2 1.4 copy-start.6
  138.5 6.7 %collective-permute-start = (f32[8,4,2,32,256]{4,3,2,1,0:T(8,128)}, f32[8,4,2,32,256]{4,3,2,1,0:T(8,128)S(1)}, u32[]{:S(2)}, u32[]{:S(2)}) collective-permute-start(f32[8,4,2,32,256]{4,3,2,1,0:T(8,128)} %get-tuple-element.27), channel_id=1, source_target_pairs={{0,64},{64,0},{1,65},{65,1},{2,66},{66,2},{3,67},{67,3},{4,68},{68... | collective-permute-start | bytes 6291464 | tf_op jit(solution)/shard_map/ppermute | solution.py:274
  194.2 12.8 %all-to-all-start.6 = ((f32[8,8,1024]{2,1,0:T(8,128)}), f32[8,8,1024]{2,1,0:T(8,128)S(1)}, u32[]{:S(2)}, u32[]{:S(2)}) async-start(f32[8,8,1024]{2,1,0:T(8,128)} %broadcast_in_dim.26), calls=%async_computation.7 | async-start | bytes 524288 | tf_op jit(solution)/shard_map/all_to_all | solution.py:244
  208.8 36.3 %all-to-all-start.7 = ((f32[8,72,1024]{2,1,0:T(8,128)}), f32[8,72,1024]{2,1,0:T(8,128)S(1)}, u32[]{:S(2)}, u32[]{:S(2)}) async-start(f32[8,72,1024]{2,1,0:T(8,128)} %pad_maximum_fusion.1), calls=%async_computation.9 | async-start | bytes 4718592 | tf_op jit(solution)/shard_map/all_to_all | solution.py:247
  245.5 5.4 %copy-start.3 = (bf16[256,512]{1,0:T(8,128)(2,1)S(1)}, bf16[256,512]{1,0:T(8,128)(2,1)}, u32[]{:S(2)}) copy-start(bf16[256,512]{1,0:T(8,128)(2,1)} %kproj_ref.3) | copy-start | bytes 786436
  245.5 5.4 %copy-start.4 = (bf16[256,512]{1,0:T(8,128)(2,1)S(1)}, bf16[256,512]{1,0:T(8,128)(2,1)}, u32[]{:S(2)}) copy-start(bf16[256,512]{1,0:T(8,128)(2,1)} %vproj_ref.3) | copy-start | bytes 786436
  246.4 16.1 %collective-permute-start.1 = (f32[48,1024]{1,0:T(8,128)S(1)}, f32[48,1024]{1,0:T(8,128)S(1)}, u32[]{:S(2)}, u32[]{:S(2)}) collective-permute-start(f32[48,1024]{1,0:T(8,128)S(1)} %maximum_multiply_fusion), channel_id=1, source_target_pairs={{0,64},{64,0},{128,192},{192,128},{1,65},{65,1},{129,193},{193,129... | collective-permute-start | bytes 589832 | tf_op jit(solution)/shard_map/ppermute | solution.py:290
  249.1 13.4 %collective-permute-start.2 = (f32[48,1024]{1,0:T(8,128)S(1)}, f32[48,1024]{1,0:T(8,128)S(1)}, u32[]{:S(2)}, u32[]{:S(2)}) collective-permute-start(f32[48,1024]{1,0:T(8,128)S(1)} %maximum_multiply_fusion), channel_id=1, source_target_pairs={{0,128},{64,192},{128,0},{192,64},{1,129},{65,193},{129,1},{193,65... | collective-permute-start | bytes 589832 | tf_op jit(solution)/shard_map/ppermute | solution.py:290
  249.5 13.0 %collective-permute-start.3 = (f32[48,1024]{1,0:T(8,128)S(1)}, f32[48,1024]{1,0:T(8,128)S(1)}, u32[]{:S(2)}, u32[]{:S(2)}) collective-permute-start(f32[48,1024]{1,0:T(8,128)S(1)} %maximum_multiply_fusion), channel_id=1, source_target_pairs={{0,192},{64,128},{128,64},{192,0},{1,193},{65,129},{129,65},{193,1... | collective-permute-start | bytes 589832 | tf_op jit(solution)/shard_map/ppermute | solution.py:290
  250.8 1.6 copy-start
  252.4 1.6 copy-start.1
  254.0 1.6 copy-start.2
  255.6 1.2 copy-start.5
Sparse Core Ops, SparseCore 0:
  16.8 41.3 reduce-scatter.2
  148.6 31.6 reduce-scatter.4

commit v5 on v4

--- a/solution.py
+++ b/solution.py
@@ -16,7 +16,6 @@
 Z = ("zh", "zl")
 NEAR = ("x", "yh")
 VMEM_LIMIT = 60 * 1024 * 1024
-LAST_VMEM = 18 * 1024 * 1024
 
 
 def dot(a, b):
@@ -219,7 +218,7 @@
         out_specs=pl.BlockSpec((rows, block), lambda i: (0, i)),
         out_shape=jax.ShapeDtypeStruct((rows, width), jnp.bfloat16),
         scratch_shapes=[pltpu.VMEM((rows, width), jnp.bfloat16)] * 2,
-        compiler_params=pltpu.CompilerParams(vmem_limit_bytes=LAST_VMEM),
+        compiler_params=pltpu.CompilerParams(vmem_limit_bytes=VMEM_LIMIT),
         cost_estimate=pl.CostEstimate(
             flops=2 * rows * width * (3 * width + both), bytes_accessed=11 << 20, transcendentals=0
         ),

time: 271 us -> 269 us (level)
  local copies, waits for them, and re-layouts: 11.1 us -> 5.47 us
  Pallas kernels: 31.9 us -> 34.7 us
    unnamed x16 -> x6, local copies, waits for them, and re-layouts: 8.11 us -> 2.45 us
    pallas_call x1, Pallas kernels: 5.69 us -> 8.55 us  [input_grads(): pl.pallas_call(functools.partial(input_grads_kernel, norm), grid=(4,), in...]
  transfers between devices with their start and end apart: 9 -> 9, of which waited for: 4 -> 5; matrix products, arithmetic and copies ran while one was open for 1% -> 1% of each run, Pallas kernels for 2% -> 3%
where the time goes in v5:
time: 269 us; the launch traced here: 268 us
  blocking collectives  108 us (40%)
  waiting for transfers between devices  75.5 us (28%)
  Pallas kernels  34.7 us (13%)
  starting transfers between devices  20.9 us (8%)
  between operations  14.2 us (5%)
  other arithmetic  8.15 us (3%)
  local copies, waits for them, and re-layouts  5.47 us (2%)
    all_to_all x2, blocking collectives, scatter_sum(): got = lax.all_to_all(part.reshape(plane, rows // plane, width), NEAR, 0, 0)  65.3 us
    all_to_all x2, waiting for transfers between devices, gather_rows(): got = lax.all_to_all(jnp.concatenate([got, extra], axis=1), NEAR, 0, 0)  62.5 us
    all_to_all x2, blocking collectives, scatter_sum(): lax.all_to_all(mine.reshape(depth, rows // plane // depth, width), Z, 0, 0)  31 us
    pallas_call x1, Pallas kernels, attend(): pl.pallas_call(functools.partial(attend_kernel, norm), grid_spec=pltpu.Pr...  16.8 us
    all_to_all x1, blocking collectives, gather_rows(): got = lax.all_to_all(jnp.broadcast_to(mine, (depth, rows, width)), Z, 0, 0)  11.9 us
    all_to_all x2, starting transfers between devices, gather_rows(): got = lax.all_to_all(jnp.concatenate([got, extra], axis=1), NEAR, 0, 0)  10.3 us
    pallas_call x1, Pallas kernels, project(): pl.pallas_call(project_kernel, grid=(n_x,), in_specs=[whole(inputs), weig...  9.36 us
    pallas_call x1, Pallas kernels, input_grads(): pl.pallas_call(functools.partial(input_grads_kernel, norm), grid=(4,), in...  8.55 us
  transfers between devices with their start and end apart: 9, of which 5 were waited for; matrix products, arithmetic and copies ran while one was open for 1% of the time, Pallas kernels for 3%

profile of v5, /device:TPU:1, one launch (start us, length us, event | category | flops | bytes accessed | tf_op | source)
XLA Modules:
  0.0 267.7 jit_solution(5852817498403051432)
XLA Ops:
  7.2 9.4 %project.1 = (bf16[512,1024]{1,0:T(8,128)(2,1)}, f32[512,1024]{1,0:T(8,128)}, bf16[1024,512]{1,0:T(8,128)(2,1)}, f32[8,4,32,512]{3,2,1,0:T(8,128)}) custom-call(bf16[512,1024]{1,0:T(8,128)(2,1)} %bitcast.59, bf16[1024,1024]{1,0:T(8,128)(2,1)} %wq_ref.3, bf16[1024,1024]{1,0:T(8,128)(2,1)} %wk_ref.3, bf16[1024,1024]{1,0:T(8,128)(2,1)} %wv_ref.3, ...), custom_call_target="tpu_custom_call" | custom-call | flops 4294967296 | bytes 14680064 | tf_op jit(solution)/shard_map/project/pallas_call | solution.py:60
  16.6 34.0 %all_to_all.40 = f32[8,64,1024]{2,1,0:T(8,128)S(1)} all-to-all(f32[8,64,1024]{2,1,0:T(8,128)} %bitcast.44), channel_id=1, replica_groups=mesh['yl'=2,'core'=2,'x'=4,'zh'=4,'zl'=2,'yh'=2] {'x','yh'}, dimensions={0} | all-to-all | bytes 4194304 | tf_op jit(solution)/shard_map/all_to_all | solution.py:233
  50.8 17.4 %all_to_all.41 = f32[8,8,1024]{2,1,0:T(8,128)S(1)} all-to-all(f32[8,8,1024]{2,1,0:T(8,128)S(1)} %bitcast.48), channel_id=1, replica_groups=mesh['yl'=2,'core'=2,'x'=4,'zh'=4,'zl'=2,'yh'=2] {'zh','zl'}, dimensions={0} | all-to-all | bytes 524288 | tf_op jit(solution)/shard_map/all_to_all | solution.py:235
  68.2 11.9 %all_to_all.42 = f32[8,8,1024]{2,1,0:T(8,128)S(1)} all-to-all(f32[8,8,1024]{2,1,0:T(8,128)S(1)} %broadcast_in_dim.23), channel_id=1, replica_groups=mesh['yl'=2,'core'=2,'x'=4,'zh'=4,'zl'=2,'yh'=2] {'zh','zl'}, dimensions={0} | all-to-all | bytes 524288 | tf_op jit(solution)/shard_map/all_to_all | solution.py:243
  81.1 1.6 pad_maximum_fusion
  82.6 5.8 %all-to-all-start.3 = ((f32[8,72,1024]{2,1,0:T(8,128)}), f32[8,72,1024]{2,1,0:T(8,128)S(1)}, u32[]{:S(2)}, u32[]{:S(2)}) async-start(f32[8,72,1024]{2,1,0:T(8,128)} %pad_maximum_fusion), calls=%async_computation.4 | async-start | bytes 4718592 | tf_op jit(solution)/shard_map/all_to_all | solution.py:246
  88.5 31.7 %all-to-all-done.3.ks_ref.vs_ref = f32[8,72,1024]{2,1,0:T(8,128)S(1)} async-done(((f32[8,72,1024]{2,1,0:T(8,128)}), f32[8,72,1024]{2,1,0:T(8,128)S(1)}, u32[]{:S(2)}, u32[]{:S(2)}) %all-to-all-start.3) | async-done | bytes 2359328 | tf_op jit(solution)/shard_map/all_to_all | solution.py:246
  120.2 1.4 copy-done.1
  121.6 16.8 %attend.1 = (bf16[512,1024]{1,0:T(8,128)(2,1)}, bf16[512,1024]{1,0:T(8,128)(2,1)}, f32[512,1024]{1,0:T(8,128)}, f32[8,4,2,32,256]{4,3,2,1,0:T(8,128)}, f32[8,4,2,32,256]{4,3,2,1,0:T(8,128)}) custom-call(s32[1]{0:T(128)} %bitcast.core_ref, bf16[512,1024]{1,0:T(8,128)(2,1)} %get-tuple-element.18.q_ref, bf16[512,1024]{1,0:T(8,128)(2,1)} %bitcast.60, ...), custom_call_target="tpu_custom_call" | custom-call | flops 6442450944 | bytes 12582912 | tf_op jit(solution)/shard_map/attend/pallas_call | solution.py:148
  138.4 2.7 collective-permute-start
  141.0 4.0 %collective-permute-done = f32[8,4,2,32,256]{4,3,2,1,0:T(8,128)S(1)} collective-permute-done((f32[8,4,2,32,256]{4,3,2,1,0:T(8,128)}, f32[8,4,2,32,256]{4,3,2,1,0:T(8,128)S(1)}, u32[]{:S(2)}, u32[]{:S(2)}) %collective-permute-start) | collective-permute-done | bytes 2097184 | tf_op jit(solution)/shard_map/ppermute | solution.py:273
  145.0 3.4 %add.22 = f32[8,4,2,32,256]{4,3,2,1,0:T(8,128)} add(f32[8,4,2,32,256]{4,3,2,1,0:T(8,128)} %get-tuple-element.26, f32[8,4,2,32,256]{4,3,2,1,0:T(8,128)S(1)} %collective-permute-done) | non-fusion elementwise | flops 524288 | bytes 6291456 | tf_op jit(solution)/shard_map/add | solution.py:273
  148.4 31.2 %all_to_all.43 = f32[8,64,1024]{2,1,0:T(8,128)S(1)} all-to-all(f32[8,64,1024]{2,1,0:T(8,128)} %bitcast.42), channel_id=1, replica_groups=mesh['yl'=2,'core'=2,'x'=4,'zh'=4,'zl'=2,'yh'=2] {'x','yh'}, dimensions={0} | all-to-all | bytes 4194304 | tf_op jit(solution)/shard_map/all_to_all | solution.py:233
  179.8 13.6 %all_to_all.44 = f32[8,8,1024]{2,1,0:T(8,128)S(1)} all-to-all(f32[8,8,1024]{2,1,0:T(8,128)S(1)} %bitcast.49), channel_id=1, replica_groups=mesh['yl'=2,'core'=2,'x'=4,'zh'=4,'zl'=2,'yh'=2] {'zh','zl'}, dimensions={0} | all-to-all | bytes 524288 | tf_op jit(solution)/shard_map/all_to_all | solution.py:235
  194.1 3.4 %all-to-all-start.6 = ((f32[8,8,1024]{2,1,0:T(8,128)}), f32[8,8,1024]{2,1,0:T(8,128)S(1)}, u32[]{:S(2)}, u32[]{:S(2)}) async-start(f32[8,8,1024]{2,1,0:T(8,128)} %broadcast_in_dim.26), calls=%async_computation.7 | async-start | bytes 524288 | tf_op jit(solution)/shard_map/all_to_all | solution.py:243
  197.5 1.0 copy.15
  198.5 8.4 %all-to-all-done.6 = f32[8,8,1024]{2,1,0:T(8,128)S(1)} async-done(((f32[8,8,1024]{2,1,0:T(8,128)}), f32[8,8,1024]{2,1,0:T(8,128)S(1)}, u32[]{:S(2)}, u32[]{:S(2)}) %all-to-all-start.6) | async-done | bytes 262176 | tf_op jit(solution)/shard_map/all_to_all | solution.py:243
  207.1 1.6 pad_maximum_fusion.1
  208.7 4.5 %all-to-all-start.7 = ((f32[8,72,1024]{2,1,0:T(8,128)}), f32[8,72,1024]{2,1,0:T(8,128)S(1)}, u32[]{:S(2)}, u32[]{:S(2)}) async-start(f32[8,72,1024]{2,1,0:T(8,128)} %pad_maximum_fusion.1), calls=%async_computation.9 | async-start | bytes 4718592 | tf_op jit(solution)/shard_map/all_to_all | solution.py:246
  213.2 1.0 slice_reduce_fusion
  214.2 30.9 %all-to-all-done.7.sums_ref = f32[8,72,1024]{2,1,0:T(8,128)S(1)} async-done(((f32[8,72,1024]{2,1,0:T(8,128)}), f32[8,72,1024]{2,1,0:T(8,128)S(1)}, u32[]{:S(2)}, u32[]{:S(2)}) %all-to-all-start.7) | async-done | bytes 2359328 | tf_op jit(solution)/shard_map/all_to_all | solution.py:246
  246.6 2.7 %collective-permute-start.1 = (f32[48,1024]{1,0:T(8,128)S(1)}, f32[48,1024]{1,0:T(8,128)S(1)}, u32[]{:S(2)}, u32[]{:S(2)}) collective-permute-start(f32[48,1024]{1,0:T(8,128)S(1)} %maximum_multiply_fusion), channel_id=1, source_target_pairs={{0,64},{64,0},{128,192},{192,128},{1,65},{65,1},{129,193},{193,129... | collective-permute-start | bytes 589832 | tf_op jit(solution)/shard_map/ppermute | solution.py:289
  249.7 1.3 collective-permute-start.3
  251.0 8.5 %input_grads.1 = bf16[512,1024]{1,0:T(8,128)(2,1)} custom-call(f32[8,72,1024]{2,1,0:T(8,128)} %copy-done, bf16[512,1024]{1,0:T(8,128)(2,1)} %get-tuple-element.30.dq_ref, bf16[256,512]{1,0:T(8,128)(2,1)} %kproj_ref.3, bf16[256,512]{1,0:T(8,128)(2,1)} %vproj_ref.3, bf16[1024,1024]{1,0:T(8,128)(2,1)} %wq_ref.3, bf16[1024,1024]{1,0:T(8,128)(2,1)} %wk_ref.3, ...), custom_call_target="tpu_custom_call" | custom-call | flops 3758096384 | bytes 11534336 | tf_op jit(solution)/shard_map/input_grads/pallas_call | solution.py:206
  (39 shorter events, 5.6 us)
Async XLA Ops:
  7.2 72.9 %reduce-scatter.3.cloned.1.call-start = ((), (), s32[]{:S(2)}) async-start(), calls=%async_computation.10 | async-start | bytes 2359296 | tf_op jit(solution)/shard_map/reduce_scatter | solution.py:251
  80.1 1.0 copy-start.2
  82.6 37.5 %all-to-all-start.3 = ((f32[8,72,1024]{2,1,0:T(8,128)}), f32[8,72,1024]{2,1,0:T(8,128)S(1)}, u32[]{:S(2)}, u32[]{:S(2)}) async-start(f32[8,72,1024]{2,1,0:T(8,128)} %pad_maximum_fusion), calls=%async_computation.4 | async-start | bytes 4718592 | tf_op jit(solution)/shard_map/all_to_all | solution.py:246
  88.4 109.1 %reduce-scatter.5.cloned.1.call-start = ((), (), s32[]{:S(2)}) async-start(), calls=%async_computation.11 | async-start | bytes 2359296 | tf_op jit(solution)/shard_map/reduce_scatter | solution.py:251
  120.2 1.4 copy-start.1
  138.4 6.7 %collective-permute-start = (f32[8,4,2,32,256]{4,3,2,1,0:T(8,128)}, f32[8,4,2,32,256]{4,3,2,1,0:T(8,128)S(1)}, u32[]{:S(2)}, u32[]{:S(2)}) collective-permute-start(f32[8,4,2,32,256]{4,3,2,1,0:T(8,128)} %get-tuple-element.27), channel_id=1, source_target_pairs={{0,64},{64,0},{1,65},{65,1},{2,66},{66,2},{3,67},{67,3},{4,68},{68... | collective-permute-start | bytes 6291464 | tf_op jit(solution)/shard_map/ppermute | solution.py:273
  194.1 12.8 %all-to-all-start.6 = ((f32[8,8,1024]{2,1,0:T(8,128)}), f32[8,8,1024]{2,1,0:T(8,128)S(1)}, u32[]{:S(2)}, u32[]{:S(2)}) async-start(f32[8,8,1024]{2,1,0:T(8,128)} %broadcast_in_dim.26), calls=%async_computation.7 | async-start | bytes 524288 | tf_op jit(solution)/shard_map/all_to_all | solution.py:243
  208.7 36.3 %all-to-all-start.7 = ((f32[8,72,1024]{2,1,0:T(8,128)}), f32[8,72,1024]{2,1,0:T(8,128)S(1)}, u32[]{:S(2)}, u32[]{:S(2)}) async-start(f32[8,72,1024]{2,1,0:T(8,128)} %pad_maximum_fusion.1), calls=%async_computation.9 | async-start | bytes 4718592 | tf_op jit(solution)/shard_map/all_to_all | solution.py:246
  245.0 1.4 copy-start
  246.6 13.0 %collective-permute-start.1 = (f32[48,1024]{1,0:T(8,128)S(1)}, f32[48,1024]{1,0:T(8,128)S(1)}, u32[]{:S(2)}, u32[]{:S(2)}) collective-permute-start(f32[48,1024]{1,0:T(8,128)S(1)} %maximum_multiply_fusion), channel_id=1, source_target_pairs={{0,64},{64,0},{128,192},{192,128},{1,65},{65,1},{129,193},{193,129... | collective-permute-start | bytes 589832 | tf_op jit(solution)/shard_map/ppermute | solution.py:289
  249.3 10.3 %collective-permute-start.2 = (f32[48,1024]{1,0:T(8,128)S(1)}, f32[48,1024]{1,0:T(8,128)S(1)}, u32[]{:S(2)}, u32[]{:S(2)}) collective-permute-start(f32[48,1024]{1,0:T(8,128)S(1)} %maximum_multiply_fusion), channel_id=1, source_target_pairs={{0,128},{64,192},{128,0},{192,64},{1,129},{65,193},{129,1},{193,65... | collective-permute-start | bytes 589832 | tf_op jit(solution)/shard_map/ppermute | solution.py:289
  249.7 10.5 %collective-permute-start.3 = (f32[48,1024]{1,0:T(8,128)S(1)}, f32[48,1024]{1,0:T(8,128)S(1)}, u32[]{:S(2)}, u32[]{:S(2)}) collective-permute-start(f32[48,1024]{1,0:T(8,128)S(1)} %maximum_multiply_fusion), channel_id=1, source_target_pairs={{0,192},{64,128},{128,64},{192,0},{1,193},{65,129},{129,65},{193,1... | collective-permute-start | bytes 589832 | tf_op jit(solution)/shard_map/ppermute | solution.py:289
Sparse Core Ops, SparseCore 0:
  16.7 41.3 reduce-scatter.2
  148.5 31.6 reduce-scatter.4

commit v6 on v5

--- a/solution.py
+++ b/solution.py
@@ -172,7 +172,7 @@
             jax.ShapeDtypeStruct(terms, jnp.float32),
             jax.ShapeDtypeStruct(terms, jnp.float32),
         ],
-        compiler_params=pltpu.CompilerParams(vmem_limit_bytes=VMEM_LIMIT),
+        compiler_params=pltpu.CompilerParams(vmem_limit_bytes=VMEM_LIMIT - 3 * 1024 * 1024),
         cost_estimate=pl.CostEstimate(
             flops=8 * rows * width * proj * 6, bytes_accessed=12 << 20, transcendentals=rows * HEADS * proj
         ),

time: 269 us -> 269 us (level)
  no operation moved by 1% of the time
where the time goes in v6:
time: 269 us; the launch traced here: 268 us
  blocking collectives  108 us (40%)
  waiting for transfers between devices  75.5 us (28%)
  Pallas kernels  34.7 us (13%)
  starting transfers between devices  20.9 us (8%)
  between operations  14.2 us (5%)
  other arithmetic  8.15 us (3%)
  local copies, waits for them, and re-layouts  5.47 us (2%)
    all_to_all x2, blocking collectives, scatter_sum(): got = lax.all_to_all(part.reshape(plane, rows // plane, width), NEAR, 0, 0)  65.3 us
    all_to_all x2, waiting for transfers between devices, gather_rows(): got = lax.all_to_all(jnp.concatenate([got, extra], axis=1), NEAR, 0, 0)  62.5 us
    all_to_all x2, blocking collectives, scatter_sum(): lax.all_to_all(mine.reshape(depth, rows // plane // depth, width), Z, 0, 0)  31 us
    pallas_call x1, Pallas kernels, attend(): pl.pallas_call(functools.partial(attend_kernel, norm), grid_spec=pltpu.Pr...  16.8 us
    all_to_all x1, blocking collectives, gather_rows(): got = lax.all_to_all(jnp.broadcast_to(mine, (depth, rows, width)), Z, 0, 0)  11.9 us
    all_to_all x2, starting transfers between devices, gather_rows(): got = lax.all_to_all(jnp.concatenate([got, extra], axis=1), NEAR, 0, 0)  10.3 us
    pallas_call x1, Pallas kernels, project(): pl.pallas_call(project_kernel, grid=(n_x,), in_specs=[whole(inputs), weig...  9.36 us
    pallas_call x1, Pallas kernels, input_grads(): pl.pallas_call(functools.partial(input_grads_kernel, norm), grid=(4,), in...  8.55 us
  transfers between devices with their start and end apart: 9, of which 5 were waited for; matrix products, arithmetic and copies ran while one was open for 1% of the time, Pallas kernels for 3%

profile of v6, /device:TPU:1, one launch (start us, length us, event | category | flops | bytes accessed | tf_op | source)
XLA Modules:
  0.0 267.7 jit_solution(5852817498403051432)
XLA Ops:
  7.2 9.4 %project.1 = (bf16[512,1024]{1,0:T(8,128)(2,1)}, f32[512,1024]{1,0:T(8,128)}, bf16[1024,512]{1,0:T(8,128)(2,1)}, f32[8,4,32,512]{3,2,1,0:T(8,128)}) custom-call(bf16[512,1024]{1,0:T(8,128)(2,1)} %bitcast.59, bf16[1024,1024]{1,0:T(8,128)(2,1)} %wq_ref.3, bf16[1024,1024]{1,0:T(8,128)(2,1)} %wk_ref.3, bf16[1024,1024]{1,0:T(8,128)(2,1)} %wv_ref.3, ...), custom_call_target="tpu_custom_call" | custom-call | flops 4294967296 | bytes 14680064 | tf_op jit(solution)/shard_map/project/pallas_call | solution.py:60
  16.6 34.0 %all_to_all.40 = f32[8,64,1024]{2,1,0:T(8,128)S(1)} all-to-all(f32[8,64,1024]{2,1,0:T(8,128)} %bitcast.44), channel_id=1, replica_groups=mesh['yl'=2,'core'=2,'x'=4,'zh'=4,'zl'=2,'yh'=2] {'x','yh'}, dimensions={0} | all-to-all | bytes 4194304 | tf_op jit(solution)/shard_map/all_to_all | solution.py:233
  50.8 17.4 %all_to_all.41 = f32[8,8,1024]{2,1,0:T(8,128)S(1)} all-to-all(f32[8,8,1024]{2,1,0:T(8,128)S(1)} %bitcast.48), channel_id=1, replica_groups=mesh['yl'=2,'core'=2,'x'=4,'zh'=4,'zl'=2,'yh'=2] {'zh','zl'}, dimensions={0} | all-to-all | bytes 524288 | tf_op jit(solution)/shard_map/all_to_all | solution.py:235
  68.2 11.9 %all_to_all.42 = f32[8,8,1024]{2,1,0:T(8,128)S(1)} all-to-all(f32[8,8,1024]{2,1,0:T(8,128)S(1)} %broadcast_in_dim.23), channel_id=1, replica_groups=mesh['yl'=2,'core'=2,'x'=4,'zh'=4,'zl'=2,'yh'=2] {'zh','zl'}, dimensions={0} | all-to-all | bytes 524288 | tf_op jit(solution)/shard_map/all_to_all | solution.py:243
  81.1 1.6 pad_maximum_fusion
  82.6 5.8 %all-to-all-start.3 = ((f32[8,72,1024]{2,1,0:T(8,128)}), f32[8,72,1024]{2,1,0:T(8,128)S(1)}, u32[]{:S(2)}, u32[]{:S(2)}) async-start(f32[8,72,1024]{2,1,0:T(8,128)} %pad_maximum_fusion), calls=%async_computation.4 | async-start | bytes 4718592 | tf_op jit(solution)/shard_map/all_to_all | solution.py:246
  88.5 31.7 %all-to-all-done.3.ks_ref.vs_ref = f32[8,72,1024]{2,1,0:T(8,128)S(1)} async-done(((f32[8,72,1024]{2,1,0:T(8,128)}), f32[8,72,1024]{2,1,0:T(8,128)S(1)}, u32[]{:S(2)}, u32[]{:S(2)}) %all-to-all-start.3) | async-done | bytes 2359328 | tf_op jit(solution)/shard_map/all_to_all | solution.py:246
  120.2 1.4 copy-done.1
  121.6 16.8 %attend.1 = (bf16[512,1024]{1,0:T(8,128)(2,1)}, bf16[512,1024]{1,0:T(8,128)(2,1)}, f32[512,1024]{1,0:T(8,128)}, f32[8,4,2,32,256]{4,3,2,1,0:T(8,128)}, f32[8,4,2,32,256]{4,3,2,1,0:T(8,128)}) custom-call(s32[1]{0:T(128)} %bitcast.core_ref, bf16[512,1024]{1,0:T(8,128)(2,1)} %get-tuple-element.18.q_ref, bf16[512,1024]{1,0:T(8,128)(2,1)} %bitcast.60, ...), custom_call_target="tpu_custom_call" | custom-call | flops 6442450944 | bytes 12582912 | tf_op jit(solution)/shard_map/attend/pallas_call | solution.py:148
  138.4 2.7 collective-permute-start
  141.0 4.0 %collective-permute-done = f32[8,4,2,32,256]{4,3,2,1,0:T(8,128)S(1)} collective-permute-done((f32[8,4,2,32,256]{4,3,2,1,0:T(8,128)}, f32[8,4,2,32,256]{4,3,2,1,0:T(8,128)S(1)}, u32[]{:S(2)}, u32[]{:S(2)}) %collective-permute-start) | collective-permute-done | bytes 2097184 | tf_op jit(solution)/shard_map/ppermute | solution.py:273
  145.0 3.4 %add.22 = f32[8,4,2,32,256]{4,3,2,1,0:T(8,128)} add(f32[8,4,2,32,256]{4,3,2,1,0:T(8,128)} %get-tuple-element.26, f32[8,4,2,32,256]{4,3,2,1,0:T(8,128)S(1)} %collective-permute-done) | non-fusion elementwise | flops 524288 | bytes 6291456 | tf_op jit(solution)/shard_map/add | solution.py:273
  148.4 31.2 %all_to_all.43 = f32[8,64,1024]{2,1,0:T(8,128)S(1)} all-to-all(f32[8,64,1024]{2,1,0:T(8,128)} %bitcast.42), channel_id=1, replica_groups=mesh['yl'=2,'core'=2,'x'=4,'zh'=4,'zl'=2,'yh'=2] {'x','yh'}, dimensions={0} | all-to-all | bytes 4194304 | tf_op jit(solution)/shard_map/all_to_all | solution.py:233
  179.8 13.6 %all_to_all.44 = f32[8,8,1024]{2,1,0:T(8,128)S(1)} all-to-all(f32[8,8,1024]{2,1,0:T(8,128)S(1)} %bitcast.49), channel_id=1, replica_groups=mesh['yl'=2,'core'=2,'x'=4,'zh'=4,'zl'=2,'yh'=2] {'zh','zl'}, dimensions={0} | all-to-all | bytes 524288 | tf_op jit(solution)/shard_map/all_to_all | solution.py:235
  194.1 3.4 %all-to-all-start.6 = ((f32[8,8,1024]{2,1,0:T(8,128)}), f32[8,8,1024]{2,1,0:T(8,128)S(1)}, u32[]{:S(2)}, u32[]{:S(2)}) async-start(f32[8,8,1024]{2,1,0:T(8,128)} %broadcast_in_dim.26), calls=%async_computation.7 | async-start | bytes 524288 | tf_op jit(solution)/shard_map/all_to_all | solution.py:243
  197.5 1.0 copy.15
  198.5 8.4 %all-to-all-done.6 = f32[8,8,1024]{2,1,0:T(8,128)S(1)} async-done(((f32[8,8,1024]{2,1,0:T(8,128)}), f32[8,8,1024]{2,1,0:T(8,128)S(1)}, u32[]{:S(2)}, u32[]{:S(2)}) %all-to-all-start.6) | async-done | bytes 262176 | tf_op jit(solution)/shard_map/all_to_all | solution.py:243
  207.1 1.6 pad_maximum_fusion.1
  208.7 4.5 %all-to-all-start.7 = ((f32[8,72,1024]{2,1,0:T(8,128)}), f32[8,72,1024]{2,1,0:T(8,128)S(1)}, u32[]{:S(2)}, u32[]{:S(2)}) async-start(f32[8,72,1024]{2,1,0:T(8,128)} %pad_maximum_fusion.1), calls=%async_computation.9 | async-start | bytes 4718592 | tf_op jit(solution)/shard_map/all_to_all | solution.py:246
  213.2 1.0 slice_reduce_fusion
  214.2 30.9 %all-to-all-done.7.sums_ref = f32[8,72,1024]{2,1,0:T(8,128)S(1)} async-done(((f32[8,72,1024]{2,1,0:T(8,128)}), f32[8,72,1024]{2,1,0:T(8,128)S(1)}, u32[]{:S(2)}, u32[]{:S(2)}) %all-to-all-start.7) | async-done | bytes 2359328 | tf_op jit(solution)/shard_map/all_to_all | solution.py:246
  246.6 2.7 %collective-permute-start.1 = (f32[48,1024]{1,0:T(8,128)S(1)}, f32[48,1024]{1,0:T(8,128)S(1)}, u32[]{:S(2)}, u32[]{:S(2)}) collective-permute-start(f32[48,1024]{1,0:T(8,128)S(1)} %maximum_multiply_fusion), channel_id=1, source_target_pairs={{0,64},{64,0},{128,192},{192,128},{1,65},{65,1},{129,193},{193,129... | collective-permute-start | bytes 589832 | tf_op jit(solution)/shard_map/ppermute | solution.py:289
  249.7 1.3 collective-permute-start.3
  251.0 8.5 %input_grads.1 = bf16[512,1024]{1,0:T(8,128)(2,1)} custom-call(f32[8,72,1024]{2,1,0:T(8,128)} %copy-done, bf16[512,1024]{1,0:T(8,128)(2,1)} %get-tuple-element.30.dq_ref, bf16[256,512]{1,0:T(8,128)(2,1)} %kproj_ref.3, bf16[256,512]{1,0:T(8,128)(2,1)} %vproj_ref.3, bf16[1024,1024]{1,0:T(8,128)(2,1)} %wq_ref.3, bf16[1024,1024]{1,0:T(8,128)(2,1)} %wk_ref.3, ...), custom_call_target="tpu_custom_call" | custom-call | flops 3758096384 | bytes 11534336 | tf_op jit(solution)/shard_map/input_grads/pallas_call | solution.py:206
  (39 shorter events, 5.6 us)
Async XLA Ops:
  7.2 72.9 %reduce-scatter.3.cloned.1.call-start = ((), (), s32[]{:S(2)}) async-start(), calls=%async_computation.10 | async-start | bytes 2359296 | tf_op jit(solution)/shard_map/reduce_scatter | solution.py:251
  80.1 1.0 copy-start.2
  82.6 37.5 %all-to-all-start.3 = ((f32[8,72,1024]{2,1,0:T(8,128)}), f32[8,72,1024]{2,1,0:T(8,128)S(1)}, u32[]{:S(2)}, u32[]{:S(2)}) async-start(f32[8,72,1024]{2,1,0:T(8,128)} %pad_maximum_fusion), calls=%async_computation.4 | async-start | bytes 4718592 | tf_op jit(solution)/shard_map/all_to_all | solution.py:246
  88.4 109.1 %reduce-scatter.5.cloned.1.call-start = ((), (), s32[]{:S(2)}) async-start(), calls=%async_computation.11 | async-start | bytes 2359296 | tf_op jit(solution)/shard_map/reduce_scatter | solution.py:251
  120.2 1.4 copy-start.1
  138.4 6.7 %collective-permute-start = (f32[8,4,2,32,256]{4,3,2,1,0:T(8,128)}, f32[8,4,2,32,256]{4,3,2,1,0:T(8,128)S(1)}, u32[]{:S(2)}, u32[]{:S(2)}) collective-permute-start(f32[8,4,2,32,256]{4,3,2,1,0:T(8,128)} %get-tuple-element.27), channel_id=1, source_target_pairs={{0,64},{64,0},{1,65},{65,1},{2,66},{66,2},{3,67},{67,3},{4,68},{68... | collective-permute-start | bytes 6291464 | tf_op jit(solution)/shard_map/ppermute | solution.py:273
  194.1 12.8 %all-to-all-start.6 = ((f32[8,8,1024]{2,1,0:T(8,128)}), f32[8,8,1024]{2,1,0:T(8,128)S(1)}, u32[]{:S(2)}, u32[]{:S(2)}) async-start(f32[8,8,1024]{2,1,0:T(8,128)} %broadcast_in_dim.26), calls=%async_computation.7 | async-start | bytes 524288 | tf_op jit(solution)/shard_map/all_to_all | solution.py:243
  208.7 36.3 %all-to-all-start.7 = ((f32[8,72,1024]{2,1,0:T(8,128)}), f32[8,72,1024]{2,1,0:T(8,128)S(1)}, u32[]{:S(2)}, u32[]{:S(2)}) async-start(f32[8,72,1024]{2,1,0:T(8,128)} %pad_maximum_fusion.1), calls=%async_computation.9 | async-start | bytes 4718592 | tf_op jit(solution)/shard_map/all_to_all | solution.py:246
  245.0 1.4 copy-start
  246.6 13.0 %collective-permute-start.1 = (f32[48,1024]{1,0:T(8,128)S(1)}, f32[48,1024]{1,0:T(8,128)S(1)}, u32[]{:S(2)}, u32[]{:S(2)}) collective-permute-start(f32[48,1024]{1,0:T(8,128)S(1)} %maximum_multiply_fusion), channel_id=1, source_target_pairs={{0,64},{64,0},{128,192},{192,128},{1,65},{65,1},{129,193},{193,129... | collective-permute-start | bytes 589832 | tf_op jit(solution)/shard_map/ppermute | solution.py:289
  249.3 10.3 %collective-permute-start.2 = (f32[48,1024]{1,0:T(8,128)S(1)}, f32[48,1024]{1,0:T(8,128)S(1)}, u32[]{:S(2)}, u32[]{:S(2)}) collective-permute-start(f32[48,1024]{1,0:T(8,128)S(1)} %maximum_multiply_fusion), channel_id=1, source_target_pairs={{0,128},{64,192},{128,0},{192,64},{1,129},{65,193},{129,1},{193,65... | collective-permute-start | bytes 589832 | tf_op jit(solution)/shard_map/ppermute | solution.py:289
  249.7 10.5 %collective-permute-start.3 = (f32[48,1024]{1,0:T(8,128)S(1)}, f32[48,1024]{1,0:T(8,128)S(1)}, u32[]{:S(2)}, u32[]{:S(2)}) collective-permute-start(f32[48,1024]{1,0:T(8,128)S(1)} %maximum_multiply_fusion), channel_id=1, source_target_pairs={{0,192},{64,128},{128,64},{192,0},{1,193},{65,129},{129,65},{193,1... | collective-permute-start | bytes 589832 | tf_op jit(solution)/shard_map/ppermute | solution.py:289
Sparse Core Ops, SparseCore 0:
  16.7 41.3 reduce-scatter.2
  148.5 31.6 reduce-scatter.4
